TPU v7x, 256 devices: a whole 4x4x8 slice. The times are simulated.
256 devices in a mesh: tile: 64 (over z, x, core), grp: 4 (over y).
Axes of the slice: x: 4, y: 4, z: 8, core: 2. Of those that a mesh axis runs over, the one named last changes fastest.
Arguments:
- observations: bfloat16 [1048576, 256], P(('tile', 'grp')), may hold values from -6 to 6
- obs_key_weight: bfloat16 [256, 512], replicated, may hold values from -0.375 to 0.375
- obs_value_weight: bfloat16 [256, 512], replicated, may hold values from -0.375 to 0.375
- background: bfloat16 [65536, 512], P(('tile', 'grp')), may hold values from -6 to 6
- query_weight: bfloat16 [512, 512], replicated, may hold values from -2.1213203 to 2.1213203
- key_weight: bfloat16 [512, 512], replicated, may hold values from -0.25 to 0.25
- value_weight: bfloat16 [512, 512], replicated, may hold values from -0.25 to 0.25
- out_weight: bfloat16 [512, 512], replicated, may hold values from -0.25 to 0.25
- owners: int32 [256, 32], replicated, may hold values from 0 to 63, as said below
- attend_list: int32 [512, 32], P(('tile', 'grp')), may hold values from -1 to 63, as said below
- obs_count: int32 [256], replicated, may hold values from 2048 to 4096, as said below
Outputs:
- updated: bfloat16 [65536, 512], P(('tile', 'grp'))
Inputs may be any that keep to these rules, and one draw needn't show every extreme that they name: `owners`: each ingest device sends to each tile either none or exactly 1 of its blocks, in any order among its blocks; its own tile (d // 4) always gets 1. `attend_list`: every block that a device's tile owns among ingest devices of the device's grp index is named exactly once among the device's 2 rows; valid entries come first in each row, -1 marks an empty entry. `obs_count`: the valid rows of an ingest device are its leading rows.
All inputs are finite; a program needn't handle non-finite values.
Results may differ from a plain program's by a relative error of at most 0.0078.
Values may be sent and summed in bfloat16 or wider, within the bound.
A program may use at most 128 MiB of HBM per device.

v0:
```python
import math

import jax
import jax.numpy as jnp
from jax import lax
from jax.sharding import PartitionSpec as P

HEADS = 8
BLOCK = 128


SOFT_LIMIT = 20.0
EPSILON = 1e-06


def block_ranks(owner_rows):
    count = owner_rows.shape[-1]
    positions = jnp.arange(count, dtype=jnp.int32)
    same_owner = owner_rows[..., :, None] == owner_rows[..., None, :]
    earlier = positions[None, :] < positions[:, None]
    return jnp.sum((same_owner & earlier).astype(jnp.int32), axis=-1)


def located_block(owner_rows, tile_index, rank_of):
    positions = jnp.arange(owner_rows.shape[-1], dtype=jnp.int32)
    matches = (owner_rows == tile_index) & (block_ranks(owner_rows) == rank_of[..., None])
    return jnp.sum(jnp.where(matches, positions, 0), axis=-1)


def attend_piece(queries, all_keys, all_values, allowed, numerator, totals):
    scores = jnp.einsum(
        "rhe,khe->hrk", queries, all_keys, preferred_element_type=jnp.float32
    ) / math.sqrt(queries.shape[-1])
    capped = SOFT_LIMIT * jnp.tanh(scores / SOFT_LIMIT)
    weights = jnp.where(allowed[None, None, :], jnp.exp(capped), jnp.float32(0.0))
    totals = totals + jnp.sum(weights, axis=-1)
    numerator = numerator + jnp.einsum(
        "hrk,khe->hre", weights.astype(jnp.bfloat16), all_values, preferred_element_type=jnp.float32
    )
    return (numerator, totals)


def local(
    observations,
    obs_key_weight,
    obs_value_weight,
    background,
    query_weight,
    key_weight,
    value_weight,
    out_weight,
    owners,
    attend_list,
    obs_count,
):
    tile_count = lax.axis_size("tile")
    group_count = lax.axis_size("grp")
    obs_blocks = observations.shape[0] // BLOCK
    channels = observations.shape[1]
    model_width = query_weight.shape[1]
    head_count = HEADS
    head_size = model_width // head_count
    query_rows = background.shape[0]
    query_blocks = query_rows // BLOCK
    entries = attend_list.shape[1]
    capacity = max(1, (2 * obs_blocks + tile_count - 1) // tile_count)
    slot_count = tile_count * capacity
    my_tile = lax.axis_index("tile")
    my_group = lax.axis_index("grp")
    my_device = my_tile * group_count + my_group
    my_owners = lax.dynamic_index_in_dim(owners, my_device, 0, keepdims=False)
    my_slots = my_owners * capacity + block_ranks(my_owners)
    placing = (my_slots[:, None] == jnp.arange(slot_count, dtype=jnp.int32)[None, :]).astype(
        jnp.bfloat16
    )
    obs_weight = jnp.concatenate([obs_key_weight, obs_value_weight], axis=1)
    packed = jnp.einsum(
        "ks,kx->sx",
        placing,
        observations.reshape(obs_blocks, BLOCK * channels),
        preferred_element_type=jnp.bfloat16,
    )
    packed = packed.reshape(tile_count, capacity, BLOCK, channels)
    received = jnp.einsum(
        "tcbx,xy->tcby",
        lax.all_to_all(packed, "tile", split_axis=0, concat_axis=0, tiled=True),
        obs_weight,
        preferred_element_type=jnp.float32,
    ).astype(jnp.bfloat16)
    received = received.reshape(slot_count, BLOCK, 2 * model_width)
    present = attend_list >= 0
    slot_ids = jnp.maximum(attend_list, 0)
    source_device = slot_ids // capacity * group_count + my_group
    source_owners = jnp.take(owners, source_device, axis=0)
    block_index = located_block(source_owners, my_tile, slot_ids % capacity)
    row_limit = jnp.take(obs_count, source_device)
    row_index = block_index[..., None] * BLOCK + jnp.arange(BLOCK, dtype=jnp.int32)[None, None, :]
    row_ok = present[..., None] & (row_index < row_limit[..., None])
    latent_weight = jnp.concatenate([key_weight, value_weight], axis=1)
    queries = jnp.dot(background, query_weight, preferred_element_type=jnp.float32).astype(
        jnp.bfloat16
    )
    queries = queries.reshape(query_rows, head_count, head_size)
    tile_pairs = jnp.dot(
        lax.all_gather(background, "grp", axis=0, tiled=True),
        latent_weight,
        preferred_element_type=jnp.float32,
    ).astype(jnp.bfloat16)
    tile_keys = tile_pairs[:, :model_width].reshape(-1, head_count, head_size)
    tile_values = tile_pairs[:, model_width:].reshape(-1, head_count, head_size)
    numerator = jnp.zeros((head_count, query_rows, head_size), jnp.float32)
    totals = jnp.zeros((head_count, query_rows), jnp.float32)
    numerator, totals = attend_piece(
        queries, tile_keys, tile_values, jnp.full((tile_keys.shape[0],), True), numerator, totals
    )
    piece_blocks = max((candidate for candidate in range(1, 9) if entries % candidate == 0))
    turn_count = entries // piece_blocks
    results = []
    for query_block in range(query_blocks):
        lower = query_block * BLOCK
        block_queries = queries[lower : lower + BLOCK]
        block_slots = slot_ids[query_block]
        block_rows = row_ok[query_block]

        def one_piece(
            step_index,
            running,
            block_queries=block_queries,
            block_slots=block_slots,
            block_rows=block_rows,
        ):
            chosen = lax.dynamic_slice_in_dim(
                block_slots, step_index * piece_blocks, piece_blocks, 0
            )
            key_value = jnp.take(received, chosen, axis=0).reshape(
                piece_blocks * BLOCK, 2 * model_width
            )
            allowed = lax.dynamic_slice_in_dim(
                block_rows, step_index * piece_blocks, piece_blocks, 0
            ).reshape(piece_blocks * BLOCK)
            piece_keys = key_value[:, :model_width].reshape(-1, head_count, head_size)
            piece_values = key_value[:, model_width:].reshape(-1, head_count, head_size)
            return attend_piece(
                block_queries, piece_keys, piece_values, allowed, running[0], running[1]
            )

        start_state = (numerator[:, lower : lower + BLOCK], totals[:, lower : lower + BLOCK])
        results.append(lax.fori_loop(0, turn_count, one_piece, start_state))
    numerator = jnp.concatenate([result[0] for result in results], axis=1)
    totals = jnp.concatenate([result[1] for result in results], axis=1)
    mixture = (numerator / totals[..., None]).transpose(1, 0, 2).reshape(query_rows, model_width)
    normed = (
        mixture * lax.rsqrt(jnp.mean(mixture * mixture, axis=-1, keepdims=True) + EPSILON)
    ).astype(jnp.bfloat16)
    return (
        background.astype(jnp.float32)
        + jnp.dot(normed, out_weight, preferred_element_type=jnp.float32)
    ).astype(jnp.bfloat16)


def solution(mesh):
    in_specs = (
        P(("tile", "grp"), None),
        P(),
        P(),
        P(("tile", "grp"), None),
        P(),
        P(),
        P(),
        P(),
        P(),
        P(("tile", "grp"), None),
        P(),
    )
    out_specs = P(("tile", "grp"), None)
    return jax.shard_map(local, mesh=mesh, in_specs=in_specs, out_specs=out_specs, check_vma=False)
```

profile of v0, /device:TPU:1, one launch (start us, length us, event | category | flops | bytes accessed | tf_op | source)
XLA Modules:
  0.0 243.0 jit_solution(15767196742128434526)
XLA Ops:
  6.5 2.9 %reshape.156 = bf16[32,32768]{1,0:T(8,128)(2,1)S(1)} reshape(bf16[4096,256]{1,0:T(8,128)(2,1)} %param.17) | data formatting | bytes 4194304 | tf_op jit(solution)/shard_map/reshape | solution.py:80
  9.9 1.4 convolution_bitcast_fusion
  11.3 4.4 %copy.56 = bf16[64,1,128,256]{3,2,1,0:T(8,128)(2,1)} copy(bf16[64,1,128,256]{3,0,2,1:T(8,128)(2,1)S(1)} %convolution_bitcast_fusion) | data formatting | bytes 8388608 | tf_op jit(solution)/shard_map/ks,kx->sx/dot_general | solution.py:77
  15.6 13.3 %all-to-all-start = ((bf16[64,1,128,256]{3,2,1,0:T(8,128)(2,1)}), bf16[64,1,128,256]{3,2,1,0:T(8,128)(2,1)}, u32[]{:S(2)}, u32[]{:S(2)}) async-start(bf16[64,1,128,256]{3,2,1,0:T(8,128)(2,1)} %copy.56), calls=%async_computation | async-start | bytes 8388608 | tf_op jit(solution)/shard_map/all_to_all | solution.py:86
  32.9 1.4 convert_reduce_fusion
  35.2 23.3 %all-gather.2.cloned.1.call-done = bf16[1024,512]{1,0:T(8,128)(2,1)} async-done(((bf16[256,512]{1,0:T(8,128)(2,1)}), bf16[1024,512]{1,0:T(8,128)(2,1)}) %all-gather.2.cloned.1.call-update) | async-done | bytes 1048592 | tf_op jit(solution)/shard_map/all_gather | solution.py:105
  58.4 2.5 %convert_bitcast_fusion = bf16[1024,1024]{0,1:T(8,128)(2,1)S(1)} fusion(bf16[1024,512]{1,0:T(8,128)(2,1)} %all-gather.2.cloned.1.call-done, bf16[512,512]{1,0:T(8,128)(2,1)S(1)} %copy-done.14, bf16[512,512]{1,0:T(8,128)(2,1)S(1)} %copy-done.15), kind=kOutput, calls=%fused_computation.41 | convolution fusion | flops 1076887552 | bytes 4194304 | tf_op jit(solution)/shard_map/dot_general | solution.py:104
  61.1 3.0 %fusion.12 = (f32[8,256]{1,0:T(8,128)S(1)}, f32[8,256,1024]{2,1,0:T(8,128)S(1)}) fusion(bf16[256,8,64]{0,2,1:T(8,128)(2,1)S(1)} %bitcast.124, bf16[1024,8,64]{0,2,1:T(8,128)(2,1)S(1)} %bitcast.122), kind=kOutput, calls=%fused_computation.34 | convolution fusion | flops 274724864 | bytes 9707520 | tf_op jit(solution)/shard_map/rhe,khe->hrk/dot_general | solution.py:31
  64.2 2.6 %fusion.15 = f32[8,256,64]{1,2,0:T(8,128)S(1)} fusion(bf16[1024,8,64]{0,2,1:T(8,128)(2,1)S(1)} %bitcast.121, f32[8,256,1024]{2,1,0:T(8,128)S(1)} %get-tuple-element.437), kind=kOutput, calls=%fused_computation.37 | convolution fusion | flops 274726912 | bytes 9961472 | tf_op jit(solution)/shard_map/hrk,khe->hre/dot_general | solution.py:37
  66.9 56.5 %all-to-all-done = bf16[64,1,128,256]{3,2,1,0:T(8,128)(2,1)} async-done(((bf16[64,1,128,256]{3,2,1,0:T(8,128)(2,1)}), bf16[64,1,128,256]{3,2,1,0:T(8,128)(2,1)}, u32[]{:S(2)}, u32[]{:S(2)}) %all-to-all-start) | async-done | bytes 4194336 | tf_op jit(solution)/shard_map/all_to_all | solution.py:86
  123.4 10.5 %convolution_convert_fusion = bf16[64,128,1024]{2,1,0:T(8,128)(2,1)} fusion(bf16[64,1,128,256]{3,2,1,0:T(8,128)(2,1)} %all-to-all-done, bf16[256,512]{1,0:T(8,128)(2,1)S(1)} %copy-done.6, bf16[256,512]{1,0:T(8,128)(2,1)S(1)} %copy-done.7), kind=kOutput, calls=%fused_computation.32 | convolution fusion | flops 4304404480 | bytes 21495808 | tf_op jit(solution)/shard_map/tcbx,xy->tcby/dot_general | solution.py:84
  133.9 50.8 %while.35 = (s32[]{:T(128)}, f32[8,128,64]{1,2,0:T(8,128)S(1)}, f32[8,128]{1,0:T(8,128)S(1)}, pred[32,128]{1,0:T(8,128)(4,1)S(1)}, s32[32]{0:T(128)S(1)}, /*inde...) while((s32[]{:T(128)}, f32[8,128,64]{1,2,0:T(8,128)S(1)}, ...), condition=%wide.region_9.11_spmd, body=%wide.region_7.10_spmd.sunk | while | flops 277939264 | bytes 32138640 | solution.py:148
  134.4 6.4 %gather_fusion.1 = bf16[8,128,1024]{2,1,0:T(8,128)(2,1)S(1)} fusion(bf16[64,128,1024]{2,1,0:T(8,128)(2,1)} %get-tuple-element.575, s32[1024]{0:T(1024)S(1)} %pad_clamp_fusion.6), kind=kCustom, calls=%fused_computation.1.clone.clone.1 | custom fusion | bytes 4194336 | tf_op jit(solution)/shard_map/while/body/eval_jaxpr/jit(_take)/gather | solution.py:135
  143.2 2.0 bitcast_reduce_fusion.5
  147.1 6.4 %gather_fusion.1 = bf16[8,128,1024]{2,1,0:T(8,128)(2,1)S(1)} fusion(bf16[64,128,1024]{2,1,0:T(8,128)(2,1)} %get-tuple-element.575, s32[1024]{0:T(1024)S(1)} %pad_clamp_fusion.6), kind=kCustom, calls=%fused_computation.1.clone.clone.1 | custom fusion | bytes 4194336 | tf_op jit(solution)/shard_map/while/body/eval_jaxpr/jit(_take)/gather | solution.py:135
  155.9 2.0 bitcast_reduce_fusion.5
  159.8 6.4 %gather_fusion.1 = bf16[8,128,1024]{2,1,0:T(8,128)(2,1)S(1)} fusion(bf16[64,128,1024]{2,1,0:T(8,128)(2,1)} %get-tuple-element.575, s32[1024]{0:T(1024)S(1)} %pad_clamp_fusion.6), kind=kCustom, calls=%fused_computation.1.clone.clone.1 | custom fusion | bytes 4194336 | tf_op jit(solution)/shard_map/while/body/eval_jaxpr/jit(_take)/gather | solution.py:135
  168.6 2.0 bitcast_reduce_fusion.5
  170.6 1.4 fusion.74
  172.5 6.4 %gather_fusion.1 = bf16[8,128,1024]{2,1,0:T(8,128)(2,1)S(1)} fusion(bf16[64,128,1024]{2,1,0:T(8,128)(2,1)} %get-tuple-element.575, s32[1024]{0:T(1024)S(1)} %pad_clamp_fusion.6), kind=kCustom, calls=%fused_computation.1.clone.clone.1 | custom fusion | bytes 4194336 | tf_op jit(solution)/shard_map/while/body/eval_jaxpr/jit(_take)/gather | solution.py:135
  181.3 2.0 bitcast_reduce_fusion.5
  184.7 49.1 %while.34 = (s32[]{:T(128)}, f32[8,128,64]{1,2,0:T(8,128)S(1)}, f32[8,128]{1,0:T(8,128)S(1)}, pred[32,128]{1,0:T(8,128)(4,1)S(1)}, s32[32]{0:T(128)S(1)}, /*inde...) while((s32[]{:T(128)}, f32[8,128,64]{1,2,0:T(8,128)S(1)}, ...), condition=%wide.region_6.8_spmd, body=%wide.region_4.7_spmd.sunk | while | flops 277939264 | bytes 32137560 | solution.py:148
  184.8 6.5 %gather_fusion = bf16[8,128,1024]{2,1,0:T(8,128)(2,1)S(1)} fusion(bf16[64,128,1024]{2,1,0:T(8,128)(2,1)} %get-tuple-element.608, s32[1024]{0:T(1024)S(1)} %pad_clamp_fusion.5), kind=kCustom, calls=%fused_computation.clone.clone.1 | custom fusion | bytes 4194336 | tf_op jit(solution)/shard_map/while/body/eval_jaxpr/jit(_take)/gather | solution.py:135
  193.6 2.0 bitcast_reduce_fusion.4
  197.1 6.5 %gather_fusion = bf16[8,128,1024]{2,1,0:T(8,128)(2,1)S(1)} fusion(bf16[64,128,1024]{2,1,0:T(8,128)(2,1)} %get-tuple-element.608, s32[1024]{0:T(1024)S(1)} %pad_clamp_fusion.5), kind=kCustom, calls=%fused_computation.clone.clone.1 | custom fusion | bytes 4194336 | tf_op jit(solution)/shard_map/while/body/eval_jaxpr/jit(_take)/gather | solution.py:135
  205.9 2.0 bitcast_reduce_fusion.4
  209.4 6.5 %gather_fusion = bf16[8,128,1024]{2,1,0:T(8,128)(2,1)S(1)} fusion(bf16[64,128,1024]{2,1,0:T(8,128)(2,1)} %get-tuple-element.608, s32[1024]{0:T(1024)S(1)} %pad_clamp_fusion.5), kind=kCustom, calls=%fused_computation.clone.clone.1 | custom fusion | bytes 4194336 | tf_op jit(solution)/shard_map/while/body/eval_jaxpr/jit(_take)/gather | solution.py:135
  218.2 2.0 bitcast_reduce_fusion.4
  220.2 1.4 fusion.69
  221.7 6.5 %gather_fusion = bf16[8,128,1024]{2,1,0:T(8,128)(2,1)S(1)} fusion(bf16[64,128,1024]{2,1,0:T(8,128)(2,1)} %get-tuple-element.608, s32[1024]{0:T(1024)S(1)} %pad_clamp_fusion.5), kind=kCustom, calls=%fused_computation.clone.clone.1 | custom fusion | bytes 4194336 | tf_op jit(solution)/shard_map/while/body/eval_jaxpr/jit(_take)/gather | solution.py:135
  230.4 2.0 bitcast_reduce_fusion.4
  234.0 2.1 fusion.19
  (159 shorter events, 34.2 us)
Async XLA Ops:
  6.5 23.3 %copy-start = (bf16[512,512]{1,0:T(8,128)(2,1)S(1)}, bf16[512,512]{1,0:T(8,128)(2,1)}, u32[]{:S(2)}) copy-start(bf16[512,512]{1,0:T(8,128)(2,1)} %param.21) | copy-start | bytes 1572868
  6.5 3.0 %copy-start.9 = (s32[256,32]{0,1:T(8,128)S(1)}, s32[256,32]{0,1:T(8,128)}, u32[]{:S(2)}) copy-start(s32[256,32]{0,1:T(8,128)} %param.25) | copy-start | bytes 98308
  15.6 14.2 %copy-start.5 = (bf16[256,512]{1,0:T(8,128)(2,1)S(1)}, bf16[256,512]{1,0:T(8,128)(2,1)}, u32[]{:S(2)}) copy-start(bf16[256,512]{1,0:T(8,128)(2,1)} %param.20) | copy-start | bytes 786436
  15.6 14.6 %copy-start.13 = (s32[2,32]{1,0:T(2,128)S(1)}, s32[2,32]{1,0:T(2,128)}, u32[]{:S(2)}) copy-start(s32[2,32]{1,0:T(2,128)} %param.26) | copy-start | bytes 772
  15.6 14.8 %copy-start.2 = (s32[256]{0:T(256)S(1)}, s32[256]{0:T(256)}, u32[]{:S(2)}) copy-start(s32[256]{0:T(256)} %param.27) | copy-start | bytes 3076
  15.6 107.7 %all-to-all-start = ((bf16[64,1,128,256]{3,2,1,0:T(8,128)(2,1)}), bf16[64,1,128,256]{3,2,1,0:T(8,128)(2,1)}, u32[]{:S(2)}, u32[]{:S(2)}) async-start(bf16[64,1,128,256]{3,2,1,0:T(8,128)(2,1)} %copy.56), calls=%async_computation | async-start | bytes 8388608 | tf_op jit(solution)/shard_map/all_to_all | solution.py:86
  29.0 29.5 %copy-start.14 = (bf16[512,512]{1,0:T(8,128)(2,1)S(1)}, bf16[512,512]{1,0:T(8,128)(2,1)}, u32[]{:S(2)}) copy-start(bf16[512,512]{1,0:T(8,128)(2,1)} %param.23) | copy-start | bytes 1572868
  29.0 29.5 %copy-start.15 = (bf16[512,512]{1,0:T(8,128)(2,1)S(1)}, bf16[512,512]{1,0:T(8,128)(2,1)}, u32[]{:S(2)}) copy-start(bf16[512,512]{1,0:T(8,128)(2,1)} %param.22) | copy-start | bytes 1572868
  29.0 29.4 %all-gather.2.cloned.1.call-start = ((), (), s32[]{:S(2)}) async-start(), calls=%async_computation.1 | async-start | bytes 1310720 | tf_op jit(solution)/shard_map/all_gather | solution.py:105
  64.2 59.2 %copy-start.6 = (bf16[256,512]{1,0:T(8,128)(2,1)S(1)}, bf16[256,512]{1,0:T(8,128)(2,1)}, u32[]{:S(2)}) copy-start(bf16[256,512]{1,0:T(8,128)(2,1)} %param.19) | copy-start | bytes 786436
  64.2 59.2 %copy-start.7 = (bf16[256,512]{1,0:T(8,128)(2,1)S(1)}, bf16[256,512]{1,0:T(8,128)(2,1)}, u32[]{:S(2)}) copy-start(bf16[256,512]{1,0:T(8,128)(2,1)} %param.18) | copy-start | bytes 786436
  66.8 67.0 %copy-start.8 = (bf16[128,512]{0,1:T(8,128)(2,1)S(1)}, bf16[128,512]{0,1:T(8,128)(2,1)}, u32[]{:S(2)}) copy-start(bf16[128,512]{0,1:T(8,128)(2,1)} %copy.58) | copy-start | bytes 393220
  133.9 50.9 %copy-start.10 = (s32[32]{0:T(128)S(1)}, s32[32]{0:T(128)}, u32[]{:S(2)}) copy-start(s32[32]{0:T(128)} %get-tuple-element.585) | copy-start | bytes 388
  133.9 0.5 copy-start.11
  143.1 2.0 copy-start.3
  145.2 1.4 copy-start.12
  146.6 0.5 copy-start.11
  155.9 2.0 copy-start.3
  157.9 1.4 copy-start.12
  159.3 0.5 copy-start.11
  168.6 2.0 copy-start.3
  170.6 1.4 copy-start.12
  172.0 0.5 copy-start.11
  181.3 2.0 copy-start.3
  183.3 1.4 copy-start.12
  193.6 2.0 copy-start.4
  205.9 2.0 copy-start.4
  218.1 2.0 copy-start.4
  230.4 2.0 copy-start.4
  233.8 2.3 copy-start.1
Sparse Core Ops, SparseCore 0:
  31.6 26.7 all-gather.1
where the time goes:
time: 244 us; the launch traced here: 243 us
  local copies, waits for them, and re-layouts  80.4 us (33%)
  waiting for transfers between devices  80.4 us (33%)
  matrix products  49.2 us (20%)
  between operations  13.7 us (6%)
  starting transfers between devices  13.3 us (5%)
  other arithmetic  5.07 us (2%)
    all_to_all x1, waiting for transfers between devices, local(): lax.all_to_all(packed, 'tile', split_axis=0, concat_axis=0, tiled=True)  56.5 us
    gather x8, local copies, waits for them, and re-layouts, one_piece(): jnp.take(received, chosen, axis=0)  51.6 us
    all_gather x1, waiting for transfers between devices, local(): lax.all_gather(background, 'grp', axis=0, tiled=True)  23.3 us
    dot_general x9, matrix products, attend_piece(): jnp.einsum('rhe,khe->hrk', queries, all_keys, preferred_element_type=jnp....  19.1 us
    while x48, local copies, waits for them, and re-layouts  16.5 us
    dot_general x9, matrix products, attend_piece(): jnp.einsum('hrk,khe->hre', weights.astype(jnp.bfloat16), all_values, pref...  13.4 us
    all_to_all x1, starting transfers between devices, local(): lax.all_to_all(packed, 'tile', split_axis=0, concat_axis=0, tiled=True)  13.3 us
    dot_general x1, matrix products, local(): jnp.einsum('tcbx,xy->tcby', lax.all_to_all(packed, 'tile', split_axis=0,...  10.5 us
  transfers between devices with their start and end apart: 2, of which 2 were waited for; matrix products, arithmetic and copies ran while one was open for 6% of the time, Pallas kernels for 0%

commit v1 on v0

v1 whole, which is shorter than its diff:
```python
import functools

import jax
import jax.numpy as jnp
from jax import lax
from jax.experimental import pallas as pl
from jax.experimental.pallas import tpu as pltpu
from jax.sharding import PartitionSpec as P

HEADS = 8
HDIM = 64
BLOCK = 128
WIDTH = 512
PAIRS = HEADS // 2
SOFT_LIMIT = 20.0
EPSILON = 1e-06
LOG2E = 1.4426950408889634
NZ, NX, NC, NG = 8, 4, 2, 4
SLOTS = NZ * NX * NC
DZ_ORDER = (4, 3, 5, 2, 6, 1, 7, 0)
MESH = pl.DeviceIdType.MESH
NT = (((1,), (1,)), ((), ()))


def f32dot(a, b):
    return jnp.dot(a, b, preferred_element_type=jnp.float32)


def f32dot_nt(a, b):
    return lax.dot_general(a, b, NT, preferred_element_type=jnp.float32)


def kernel(
    send_idx,
    valid_rows,
    query_pick,
    obs_ref,
    okw_ref,
    ovw_ref,
    bg_ref,
    qw_ref,
    kw_ref,
    vw_ref,
    ow_ref,
    out_ref,
    packed,
    recv,
    bgs,
    qbd,
    ovwt,
    vwt,
    acc,
    tot,
    send_sem,
    recv_sem,
    bsend_sem,
    brecv_sem,
):
    tile = lax.axis_index("tile")
    grp = lax.axis_index("grp")
    z, x, c = tile // (NX * NC), (tile // NC) % NX, tile % NC

    def shifted(dz, o, sign):
        dx, dc = o // NC, o % NC
        zz = (z + sign * dz + NZ) % NZ
        xx = (x + sign * dx + NX) % NX
        cc = (c + dc) % NC
        return (zz * NX + xx) * NC + cc

    barrier = pltpu.get_barrier_semaphore()

    def greet(i, carry):
        pl.semaphore_signal(barrier, inc=1, device_id=((tile + i) % SLOTS, grp), device_id_type=MESH)
        return carry

    lax.fori_loop(1, SLOTS, greet, 0)
    for i in range(1, NG):
        pl.semaphore_signal(barrier, inc=1, device_id=(tile, (grp + i) % NG), device_id_type=MESH)
    pl.semaphore_wait(barrier, SLOTS - 1 + NG - 1)

    def slot_copy(i, dest):
        return pltpu.make_async_remote_copy(
            src_ref=packed.at[i],
            dst_ref=recv.at[i],
            send_sem=send_sem.at[i],
            recv_sem=recv_sem.at[i],
            device_id=(dest, grp),
            device_id_type=MESH,
        )

    def bg_copy(i):
        return pltpu.make_async_remote_copy(
            src_ref=bg_ref,
            dst_ref=bgs.at[i - 1],
            send_sem=bsend_sem.at[i - 1],
            recv_sem=brecv_sem.at[i - 1],
            device_id=(tile, (grp + i) % NG),
            device_id_type=MESH,
        )

    for i in range(1, NG):
        bg_copy(i).start()

    def send_round(o, carry):
        for pos, dz in enumerate(DZ_ORDER):
            i = o * NZ + pos
            dest = shifted(dz, o, 1)
            block = obs_ref[send_idx[dest]]
            if dz == 0:

                @pl.when(o == 0)
                def _():
                    recv[i] = block

                @pl.when(o > 0)
                def _():
                    packed[i] = block
                    slot_copy(i, dest).start()

            else:
                packed[i] = block
                slot_copy(i, dest).start()
        return carry

    lax.fori_loop(0, NX * NC, send_round, 0)

    ovwt[...] = ovw_ref[...].T
    vwt[...] = vw_ref[...].T
    qwt = qw_ref[...].T
    qt = f32dot_nt(qwt, bg_ref[...]).astype(jnp.bfloat16)
    qbd[...] = jnp.zeros_like(qbd)
    for b in range(2):
        for h in range(HEADS):
            half = h % 2
            qbd[b, h // 2, half * HDIM : (half + 1) * HDIM, half * BLOCK : (half + 1) * BLOCK] = qt[
                h * HDIM : (h + 1) * HDIM, b * BLOCK : (b + 1) * BLOCK
            ]
    acc[...] = jnp.zeros_like(acc)
    tot[...] = jnp.zeros_like(tot)

    def weigh(keys, p, pick):
        s = f32dot(keys[:, p * 2 * HDIM : (p + 1) * 2 * HDIM], qbd[pick, p])
        capped = jnp.tanh(s * (1.0 / (8.0 * SOFT_LIMIT)))
        return jnp.exp2(capped * (SOFT_LIMIT * LOG2E)).astype(jnp.bfloat16)

    def attend(keys, vt, mask_rows, p, pick):
        w = weigh(keys, p, pick)
        va = jnp.concatenate([vt[p * 2 * HDIM : (p + 1) * 2 * HDIM], mask_rows], axis=0)
        o = f32dot(va, w)
        return o[:HDIM, :BLOCK], o[HDIM : 2 * HDIM, BLOCK:], o[2 * HDIM : 2 * HDIM + 8]

    ones = jnp.ones((16, BLOCK), jnp.bfloat16)

    def latent_block(rows):
        keys = f32dot(rows, kw_ref[...]).astype(jnp.bfloat16)
        vt = f32dot_nt(vwt[...], rows).astype(jnp.bfloat16)
        for b in range(2):
            for p in range(PAIRS):
                top, low, total = attend(keys, vt, ones, p, b)
                acc[b, 2 * p] += top
                acc[b, 2 * p + 1] += low
                tot[b, p] += total

    def own_latents(j, carry):
        latent_block(bg_ref[pl.ds(pl.multiple_of(j * BLOCK, BLOCK), BLOCK), :])
        return carry

    lax.fori_loop(0, 2, own_latents, 0)

    def slot_step(i, carry):
        o, pos = i // NZ, i % NZ
        dz = jnp.where(pos == 0, 4, jnp.where(pos == 7, 0, jnp.where(pos % 2 == 1, 4 - (pos + 1) // 2, 4 + pos // 2)))
        source = shifted(dz, o, -1)

        @pl.when(i != NZ - 1)
        def _():
            slot_copy(i, tile).wait_recv()

        rows_ok = valid_rows[source]
        pick = query_pick[source]
        row_id = lax.broadcasted_iota(jnp.int32, (BLOCK, obs_ref.shape[2]), 0)
        block = recv[i]
        block = jnp.where(row_id < rows_ok, block, jnp.zeros_like(block))
        lane_id = lax.broadcasted_iota(jnp.int32, (16, BLOCK), 1)
        mask_rows = jnp.where(lane_id < rows_ok, 1.0, 0.0).astype(jnp.bfloat16)
        keys = f32dot(block, okw_ref[...]).astype(jnp.bfloat16)
        vt = f32dot_nt(ovwt[...], block).astype(jnp.bfloat16)
        first = pick == 0
        for p in range(PAIRS):
            top, low, total = attend(keys, vt, mask_rows, p, pick)
            for b in range(2):
                mine = first if b == 0 else jnp.logical_not(first)
                acc[b, 2 * p] += jnp.where(mine, top, 0.0)
                acc[b, 2 * p + 1] += jnp.where(mine, low, 0.0)
                tot[b, p] += jnp.where(mine, total, 0.0)
        return carry

    lax.fori_loop(0, NZ, slot_step, 0)
    for i in range(1, NG):
        bg_copy(i).wait_recv()

        def other_latents(j, carry, i=i):
            latent_block(bgs[i - 1, pl.ds(pl.multiple_of(j * BLOCK, BLOCK), BLOCK), :])
            return carry

        lax.fori_loop(0, 2, other_latents, 0)
    lax.fori_loop(NZ, SLOTS, slot_step, 0)

    for b in range(2):
        parts = []
        for h in range(HEADS):
            total = tot[b, h // 2, 0:1, (h % 2) * BLOCK : (h % 2 + 1) * BLOCK]
            parts.append(acc[b, h] / total)
        mixture = jnp.concatenate(parts, axis=0)
        scale = lax.rsqrt(jnp.mean(mixture * mixture, axis=0, keepdims=True) + EPSILON)
        normed = (mixture * scale).T.astype(jnp.bfloat16)
        rows = slice(b * BLOCK, (b + 1) * BLOCK)
        out_ref[rows, :] = (bg_ref[rows, :].astype(jnp.float32) + f32dot(normed, ow_ref[...])).astype(jnp.bfloat16)

    def finish(i, carry):
        @pl.when(i != NZ - 1)
        def _():
            slot_copy(i, tile).wait_send()

        return carry

    lax.fori_loop(0, SLOTS, finish, 0)
    for i in range(1, NG):
        bg_copy(i).wait_send()


def tables(owners, attend_list, obs_count):
    tile = lax.axis_index("tile")
    grp = lax.axis_index("grp")
    tiles = jnp.arange(SLOTS, dtype=jnp.int32)
    by_group = lax.dynamic_index_in_dim(owners.reshape(SLOTS, NG, -1), grp, 1, keepdims=False)
    counts = lax.dynamic_index_in_dim(obs_count.reshape(SLOTS, NG), grp, 1, keepdims=False)
    mine = lax.dynamic_index_in_dim(by_group, tile, 0, keepdims=False)
    blocks = jnp.arange(mine.shape[0], dtype=jnp.int32)
    send_idx = jnp.sum(jnp.where(mine[None, :] == tiles[:, None], blocks[None, :], 0), axis=1)
    owned = by_group == tile
    limits = jnp.clip(counts[:, None] - blocks[None, :] * BLOCK, 0, BLOCK)
    valid_rows = jnp.sum(jnp.where(owned, limits, 0), axis=1)
    query_pick = jnp.max((attend_list[1][None, :] == tiles[:, None]).astype(jnp.int32), axis=1)
    return send_idx, valid_rows, query_pick


def local(
    observations,
    obs_key_weight,
    obs_value_weight,
    background,
    query_weight,
    key_weight,
    value_weight,
    out_weight,
    owners,
    attend_list,
    obs_count,
):
    send_idx, valid_rows, query_pick = tables(owners, attend_list, obs_count)
    channels = observations.shape[1]
    blocks = observations.reshape(-1, BLOCK, channels)
    smem = pl.BlockSpec(memory_space=pltpu.SMEM)
    vmem = pl.BlockSpec(memory_space=pltpu.VMEM)
    bf16, f32 = jnp.bfloat16, jnp.float32
    return pl.pallas_call(
        kernel,
        out_shape=jax.ShapeDtypeStruct(background.shape, bf16),
        in_specs=[smem] * 3 + [vmem] * 8,
        out_specs=vmem,
        scratch_shapes=[
            pltpu.VMEM((SLOTS, BLOCK, channels), bf16),
            pltpu.VMEM((SLOTS, BLOCK, channels), bf16),
            pltpu.VMEM((NG - 1, 2 * BLOCK, WIDTH), bf16),
            pltpu.VMEM((2, PAIRS, 2 * HDIM, 2 * BLOCK), bf16),
            pltpu.VMEM((WIDTH, channels), bf16),
            pltpu.VMEM((WIDTH, WIDTH), bf16),
            pltpu.VMEM((2, HEADS, HDIM, BLOCK), f32),
            pltpu.VMEM((2, PAIRS, 8, 2 * BLOCK), f32),
            pltpu.SemaphoreType.DMA((SLOTS,)),
            pltpu.SemaphoreType.DMA((SLOTS,)),
            pltpu.SemaphoreType.DMA((NG - 1,)),
            pltpu.SemaphoreType.DMA((NG - 1,)),
        ],
        compiler_params=pltpu.CompilerParams(
            collective_id=0, has_side_effects=True, vmem_limit_bytes=40 * 1024 * 1024
        ),
        cost_estimate=pl.CostEstimate(flops=12_000_000_000, bytes_accessed=8_000_000, transcendentals=21_000_000),
    )(
        send_idx,
        valid_rows,
        query_pick,
        blocks,
        obs_key_weight,
        obs_value_weight,
        background,
        query_weight,
        key_weight,
        value_weight,
        out_weight,
    )


def solution(mesh):
    rows = P(("tile", "grp"), None)
    in_specs = (rows, P(), P(), rows, P(), P(), P(), P(), P(), rows, P())
    return jax.shard_map(local, mesh=mesh, in_specs=in_specs, out_specs=rows, check_vma=False)
```

time: 244 us -> 123 us (0.50)
  Pallas kernels: 0 us -> 110 us
  waiting for transfers between devices: 80.4 us -> 0 us
  local copies, waits for them, and re-layouts: 80.4 us -> 11.9 us
  matrix products: 49.2 us -> 0 us
  between operations: 13.7 us -> 0.05 us
  starting transfers between devices: 13.3 us -> 0 us
  other arithmetic: 5.07 us -> 0.2 us
    pallas_call x0 -> x1, Pallas kernels: none -> 110 us  [local(): pl.pallas_call(kernel, out_shape=jax.ShapeDtypeStruct(background.shape, b...]
    all_to_all x1 -> x0, waiting for transfers between devices: 56.5 us -> none  [local(): lax.all_to_all(packed, 'tile', split_axis=0, concat_axis=0, tiled=True)]
    gather x11 -> x0, local copies, waits for them, and re-layouts: 53.1 us -> none  [the longest x8 51.6 us: one_piece(): jnp.take(received, chosen, axis=0)]
    dot_general x23 -> x0, matrix products: 49.2 us -> none  [the longest x9 19.1 us: attend_piece(): jnp.einsum('rhe,khe->hrk', queries, all_keys, preferred_element_type=jnp....]
    all_gather x1 -> x0, waiting for transfers between devices: 23.3 us -> none  [local(): lax.all_gather(background, 'grp', axis=0, tiled=True)]
    while x48 -> x0, local copies, waits for them, and re-layouts: 16.5 us -> none
    all_to_all x1 -> x0, starting transfers between devices: 13.3 us -> none  [local(): lax.all_to_all(packed, 'tile', split_axis=0, concat_axis=0, tiled=True)]
    unnamed x25 -> x19, local copies, waits for them, and re-layouts: 0.16 us -> 10.2 us
  transfers between devices with their start and end apart: 2 -> 0, of which waited for: 2 -> 0; matrix products, arithmetic and copies ran while one was open for 6% -> 0% of each run, Pallas kernels for 0% -> 0%
where the time goes in v1:
time: 123 us; the launch traced here: 122 us
  Pallas kernels  110 us (89%)
  local copies, waits for them, and re-layouts  11.9 us (10%)
    pallas_call x1, Pallas kernels, local(): pl.pallas_call(kernel, out_shape=jax.ShapeDtypeStruct(background.shape, b...  110 us
    unnamed x19, local copies, waits for them, and re-layouts  10.2 us

profile of v1, /device:TPU:1, one launch (start us, length us, event | category | flops | bytes accessed | tf_op | source)
XLA Modules:
  0.0 122.2 jit_solution(14437616547189359107)
XLA Ops:
  0.0 0.7 slice_bitcast_fusion
  0.7 0.8 reshape.19
  1.5 0.2 dynamic-slice_reduce_fusion
  1.6 0.9 copy.19
  2.6 0.1 copy.21
  2.6 0.1 convert_reduce_fusion
  2.7 0.1 select_reduce_fusion.1.send_idx
  2.8 0.0 copy-start
  2.8 1.6 %copy-done = bf16[4096,256]{1,0:T(8,128)(2,1)S(1)} copy-done((bf16[4096,256]{1,0:T(8,128)(2,1)S(1)}, bf16[4096,256]{1,0:T(8,128)(2,1)}, u32[]{:S(2)}) %copy-start) | copy-done | bytes 2097176
  4.4 0.0 copy-start.1
  4.4 1.0 copy-done.1
  5.5 0.0 copy-start.2
  5.5 1.0 copy-done.2
  6.5 0.0 copy-start.3
  6.5 1.0 copy-done.3
  7.6 0.0 copy-start.4
  7.6 1.0 copy-done.4
  8.6 0.0 copy-start.5
  8.6 0.9 copy-done.5
  9.5 0.0 copy-start.6
  9.6 0.9 copy-done.6
  10.5 0.0 copy-start.7
  10.5 0.9 copy-done.7
  11.4 110.0 %shard_map.109 = bf16[256,512]{1,0:T(8,128)(2,1)S(1)} custom-call(s32[64]{0:T(128)S(1)} %select_reduce_fusion.1.send_idx, s32[64]{0:T(128)S(1)} %get-tuple-element.6.valid_rows, s32[64]{0:T(128)S(1)} %get-tuple-element.5.query_pick, bf16[32,128,256]{2,1,0:T(8,128)(2,1)S(1)} %bitcast.8, bf16[256,512]{1,0:T(8,128)(2,1)S(1)} %copy-done.5, ...), custom_call_target="tpu_custom_call" | custom-call | flops 12000000000 | bytes 8000000 | tf_op jit(solution)/shard_map/pallas_call | solution.py:267
  121.5 0.7 copy.23
  (3 shorter events, 0.0 us)
Async XLA Ops:
  2.8 1.6 %copy-start = (bf16[4096,256]{1,0:T(8,128)(2,1)S(1)}, bf16[4096,256]{1,0:T(8,128)(2,1)}, u32[]{:S(2)}) copy-start(bf16[4096,256]{1,0:T(8,128)(2,1)} %param.11) | copy-start | bytes 6291460
  4.4 1.0 copy-start.1
  5.5 1.0 copy-start.2
  6.5 1.0 copy-start.3
  7.6 1.0 copy-start.4
  8.6 0.9 copy-start.5
  9.5 0.9 copy-start.6
  10.5 0.9 copy-start.7

commit v2 on v0

v2 whole, which is shorter than its diff:
```python
import functools

import jax
import jax.numpy as jnp
from jax import lax
from jax.experimental import pallas as pl
from jax.experimental.pallas import tpu as pltpu
from jax.sharding import PartitionSpec as P

HEADS = 8
HDIM = 64
BLOCK = 128
WIDTH = 512
CHANNELS = 256
PAIRS = HEADS // 2
SOFT_LIMIT = 20.0
EPSILON = 1e-06
LOG2E = 1.4426950408889634
NZ, NX, NC, NG = 8, 4, 2, 4
SIDE = NX * NC
SLOTS = NZ * SIDE
RING = SLOTS * NG
STRIDE = RING // NZ
OBS_BLOCKS = 32
CHUNK = 4
CHUNKS = 10
TURNS = CHUNK * CHUNKS
LAG = 2 * CHUNK
BOUNDS = (20, 32, 40, 40)
MESH = pl.DeviceIdType.MESH
NT = (((1,), (1,)), ((), ()))


def relay_plan(owners, counts, second, tile, grp, roll):
    f32, i32 = jnp.float32, jnp.int32
    n_blk = owners.shape[0]
    z, x, c = tile // (NX * NC), (tile // NC) % NX, tile % NC
    me = tile * NG + grp
    lane = lax.broadcasted_iota(i32, (n_blk, RING), 1)
    block = lax.broadcasted_iota(i32, (n_blk, RING), 0)
    lane_row = lane[:1]

    def tally(cond):
        return jnp.sum(jnp.where(cond, 1.0, 0.0).astype(f32), axis=0, keepdims=True)

    def column(values, which):
        return jnp.sum(jnp.where(lane[: values.shape[0]] == which, values, 0.0), axis=1, keepdims=True)

    live = block * BLOCK < counts
    away = (owners // (NX * NC) - lane // STRIDE + NZ) % NZ
    side = (owners // NC) % NX
    core = owners % NC
    right = (away >= 1) & ((away < NZ // 2) | ((away == NZ // 2) & ((side + core) % 2 == 0)))
    left = (away >= NZ // 2) & jnp.logical_not(right)
    hops = jnp.where(right, away, jnp.where(left, NZ - away, 0))
    moving = live & (hops > 0)
    shift = (side - (lane // (NC * NG)) % NX + NX + NX - 1) % NX
    order = (4 - hops) * (NX * NC) + shift * NC + core + jnp.where(right, 0, 64)
    key = jnp.where(moving, order, 1000)
    rank = jnp.zeros((n_blk, RING), f32)
    for k in range(n_blk):
        other = key[k : k + 1]
        rank += jnp.where((other < key) & ((other < 64) == (key < 64)), 1.0, 0.0)
    ahead, starts, over = {}, {}, jnp.zeros((1, RING), f32)
    for d, way in enumerate((right, left)):
        turn = 1 if d == 0 else -1
        count = [tally(moving & way & (hops >= k)) for k in range(1, 5)]
        begin = [jnp.zeros((1, RING), f32)]
        for k in range(1, 4):
            length = roll(count[k - 1], turn * (k - 1) * STRIDE)
            begin.append(jnp.maximum(begin[-1] + length, roll(begin[-1], turn * STRIDE) + LAG))
        for k in range(4):
            length = roll(count[k], turn * k * STRIDE)
            over = jnp.maximum(over, begin[k] + length - BOUNDS[k])
            ahead[d, k] = length
            starts[d, k] = begin[k]
    spot = jnp.zeros((n_blk, RING), f32)
    for d, way in enumerate((right, left)):
        turn = 1 if d == 0 else -1
        for k in range(4):
            landed = roll(starts[d, k], -turn * k * STRIDE)
            spot = jnp.where(way & (hops == k + 1), landed + rank + (n_blk + d * TURNS), spot)
    blockf = block.astype(f32)
    spot = jnp.where(hops == 0, blockf, spot)
    spot = jnp.where(live, spot, -1.0)
    rows = []
    turns = lane_row.astype(f32)
    own_key, own_rank = column(key.astype(f32), me), column(rank, me)
    for d in range(2):
        turn = 1 if d == 0 else -1
        mine = (own_key < 64.0) if d == 0 else ((own_key >= 64.0) & (own_key < 1000.0))
        source = jnp.sum(jnp.where(mine & (own_rank == turns), blockf, 0.0), axis=0, keepdims=True)
        before = (me - turn * STRIDE + RING) % RING
        for k in range(1, 4):
            begin, length = column(starts[d, k], me), column(ahead[d, k], me)
            old = column(starts[d, k - 1], before)
            inside = (turns >= begin) & (turns < begin + length)
            source = jnp.where(inside, turns - begin + old + (n_blk + d * TURNS), source)
        rows.append(source)
    group = lane_row // (NX * NC)
    owner_cols = jnp.zeros((n_blk, RING), f32)
    spot_cols = jnp.zeros((n_blk, RING), f32)
    ownersf = owners.astype(f32)
    for g in range(NZ):
        dz = (g + 1) // 2 if g % 2 else (NZ - g // 2) % NZ
        origin = (me - dz * STRIDE + RING) % RING
        owner_cols = jnp.where(group == g, column(ownersf, origin), owner_cols)
        spot_cols = jnp.where(group == g, column(spot, origin), spot_cols)
    local = lane_row % (NX * NC)
    dest = (z * NX + (x + local // NC) % NX) * NC + (c + local % NC) % NC
    found = (owner_cols == dest.astype(f32)) & (spot_cols >= 0.0)
    rows.append(jnp.sum(jnp.where(found, spot_cols, 0.0), axis=0, keepdims=True))
    limits = jnp.clip(counts - block * BLOCK, 0, BLOCK).astype(f32)
    rows.append(jnp.sum(jnp.where(owners == tile, limits, 0.0), axis=0, keepdims=True))
    pick = jnp.zeros((1, RING), f32)
    for entry in second:
        pick = jnp.where(lane_row == entry, 1.0, pick)
    rows.append(pick)
    rows.append(jnp.broadcast_to(jnp.max(over, axis=1, keepdims=True), (1, RING)))
    own_owner = column(ownersf, me)
    rows.append(jnp.sum(jnp.where(own_owner == turns, blockf, 0.0), axis=0, keepdims=True))
    rows.append(jnp.zeros((1, RING), f32))
    return jnp.concatenate(rows, axis=0).astype(i32)


def plan_kernel(list_ref, owners_ref, counts_ref, out_ref):
    tile, grp = lax.axis_index("tile"), lax.axis_index("grp")
    second = [list_ref[1, k] for k in range(list_ref.shape[1])]
    out_ref[...] = relay_plan(
        owners_ref[...], counts_ref[...], second, tile, grp, lambda a, n: pltpu.roll(a, n % RING, 1)
    )


def f32dot(a, b):
    return jnp.dot(a, b, preferred_element_type=jnp.float32)


def f32dot_nt(a, b):
    return lax.dot_general(a, b, NT, preferred_element_type=jnp.float32)


class Parts:
    def __init__(self, table, hbm, out_ref, work):
        (self.obs, *self.sources) = hbm
        (self.recv, self.bgs, self.okw, self.ovw, self.qw, self.kw, self.vw, self.ow) = work[:8]
        (self.qbd, self.ovwt, self.vwt, self.acc, self.tot) = work[8:13]
        (self.load_sem, self.bsend_sem, self.brecv_sem) = work[13:]
        self.table, self.out_ref = table, out_ref
        self.tile, self.grp = lax.axis_index("tile"), lax.axis_index("grp")
        self.z, self.x, self.c = self.tile // SIDE, (self.tile // NC) % NX, self.tile % NC

    def at(self, dz, dx, dc):
        zz, xx, cc = (self.z + dz + NZ) % NZ, (self.x + dx + NX) % NX, (self.c + dc) % NC
        return (zz * NX + xx) * NC + cc

    def loads(self, obs_target):
        targets = (self.okw, self.ovw, self.bgs.at[0], self.qw, self.kw, self.vw, self.ow)
        pairs = [(self.obs, obs_target)] + list(zip(self.sources, targets))
        return [pltpu.make_async_copy(a, b, self.load_sem.at[k]) for k, (a, b) in enumerate(pairs)]

    def bg_copy(self, i):
        return pltpu.make_async_remote_copy(
            src_ref=self.bgs.at[0],
            dst_ref=self.bgs.at[i],
            send_sem=self.bsend_sem.at[i - 1],
            recv_sem=self.brecv_sem.at[i - 1],
            device_id=(self.tile, (self.grp + i) % NG),
            device_id_type=MESH,
        )

    def setup(self):
        self.ovwt[...] = self.ovw[...].T
        self.vwt[...] = self.vw[...].T
        qt = f32dot_nt(self.qw[...].T, self.bgs[0]).astype(jnp.bfloat16)
        self.qbd[...] = jnp.zeros_like(self.qbd)
        for b in range(2):
            for h in range(HEADS):
                half = h % 2
                rows, lanes = slice(half * HDIM, (half + 1) * HDIM), slice(half * BLOCK, (half + 1) * BLOCK)
                self.qbd[b, h // 2, rows, lanes] = qt[h * HDIM : (h + 1) * HDIM, b * BLOCK : (b + 1) * BLOCK]
        self.acc[...] = jnp.zeros_like(self.acc)
        self.tot[...] = jnp.zeros_like(self.tot)

    def attend(self, keys, vt, mask_rows, p, pick):
        s = f32dot(keys[:, p * 2 * HDIM : (p + 1) * 2 * HDIM], self.qbd[pick, p])
        capped = jnp.tanh(s * (1.0 / (8.0 * SOFT_LIMIT)))
        w = jnp.exp2(capped * (SOFT_LIMIT * LOG2E)).astype(jnp.bfloat16)
        va = jnp.concatenate([vt[p * 2 * HDIM : (p + 1) * 2 * HDIM], mask_rows], axis=0)
        o = f32dot(va, w)
        return o[:HDIM, :BLOCK], o[HDIM : 2 * HDIM, BLOCK:], o[2 * HDIM : 2 * HDIM + 8]

    def latent_step(self, j, carry):
        rows = self.bgs[j // 2, pl.ds(pl.multiple_of((j % 2) * BLOCK, BLOCK), BLOCK), :]
        keys = f32dot(rows, self.kw[...]).astype(jnp.bfloat16)
        vt = f32dot_nt(self.vwt[...], rows).astype(jnp.bfloat16)
        ones = jnp.ones((16, BLOCK), jnp.bfloat16)
        for b in range(2):
            for p in range(PAIRS):
                top, low, total = self.attend(keys, vt, ones, p, b)
                self.acc[b, 2 * p] += top
                self.acc[b, 2 * p + 1] += low
                self.tot[b, p] += total
        return carry

    def slot_way(self, i):
        g, o = i // SIDE, i % SIDE
        dz = jnp.where(g % 2 == 1, (g + 1) // 2, (NZ - g // 2) % NZ)
        return dz, o // NC, o % NC

    def slot_math(self, i):
        dz, dx, dc = self.slot_way(i)
        source = self.at(-dz, -dx, -dc)
        rows_ok = self.table[3, source * NG + self.grp]
        pick = self.table[4, source]
        row_id = lax.broadcasted_iota(jnp.int32, (BLOCK, CHANNELS), 0)
        block = self.recv[i]
        block = jnp.where(row_id < rows_ok, block, jnp.zeros_like(block))
        lane_id = lax.broadcasted_iota(jnp.int32, (16, BLOCK), 1)
        mask_rows = jnp.where(lane_id < rows_ok, 1.0, 0.0).astype(jnp.bfloat16)
        keys = f32dot(block, self.okw[...]).astype(jnp.bfloat16)
        vt = f32dot_nt(self.ovwt[...], block).astype(jnp.bfloat16)
        first = pick == 0
        for p in range(PAIRS):
            top, low, total = self.attend(keys, vt, mask_rows, p, pick)
            for b in range(2):
                mine = first if b == 0 else jnp.logical_not(first)
                self.acc[b, 2 * p] += jnp.where(mine, top, 0.0)
                self.acc[b, 2 * p + 1] += jnp.where(mine, low, 0.0)
                self.tot[b, p] += jnp.where(mine, total, 0.0)

    def result(self):
        for b in range(2):
            parts = []
            for h in range(HEADS):
                total = self.tot[b, h // 2, 0:1, (h % 2) * BLOCK : (h % 2 + 1) * BLOCK]
                parts.append(self.acc[b, h] / total)
            mixture = jnp.concatenate(parts, axis=0)
            scale = lax.rsqrt(jnp.mean(mixture * mixture, axis=0, keepdims=True) + EPSILON)
            normed = (mixture * scale).T.astype(jnp.bfloat16)
            rows = slice(b * BLOCK, (b + 1) * BLOCK)
            update = f32dot(normed, self.ow[...])
            self.out_ref[rows, :] = (self.bgs[0, rows, :].astype(jnp.float32) + update).astype(jnp.bfloat16)


def slot_copier(me, packed, send_sem, recv_sem):
    def slot_copy(i, dest):
        return pltpu.make_async_remote_copy(
            src_ref=packed.at[i],
            dst_ref=me.recv.at[i],
            send_sem=send_sem.at[i],
            recv_sem=recv_sem.at[i],
            device_id=(dest, me.grp),
            device_id_type=MESH,
        )

    return slot_copy


def direct_kernel(table, *refs):
    hbm, out_ref, (held, packed, send_sem, recv_sem), work = refs[:8], refs[8], refs[9:13], refs[13:]
    me = Parts(table, hbm, out_ref, work)
    loads = me.loads(held)
    for load in loads:
        load.start()
    barrier = pltpu.get_barrier_semaphore()

    def greet(i, carry):
        pl.semaphore_signal(barrier, inc=1, device_id=((me.tile + i) % SLOTS, me.grp), device_id_type=MESH)
        return carry

    lax.fori_loop(1, SLOTS, greet, 0)
    for i in range(1, NG):
        pl.semaphore_signal(barrier, inc=1, device_id=(me.tile, (me.grp + i) % NG), device_id_type=MESH)
    for load in loads:
        load.wait()
    pl.semaphore_wait(barrier, SLOTS - 1 + NG - 1)
    slot_copy = slot_copier(me, packed, send_sem, recv_sem)
    for i in range(1, NG):
        me.bg_copy(i).start()

    def send(n, carry):
        i = (n % NZ) * SIDE + n // NZ
        dest = me.at(*me.slot_way(i))
        block = held[table[6, dest]]

        @pl.when(i == 0)
        def _():
            me.recv[i] = block

        @pl.when(i > 0)
        def _():
            packed[i] = block
            slot_copy(i, dest).start()

        return carry

    lax.fori_loop(0, SLOTS, send, 0)
    me.setup()
    for i in range(1, NG):
        me.bg_copy(i).wait_recv()
    lax.fori_loop(0, 2 * NG, me.latent_step, 0)

    def step(n, carry):
        i = (n % NZ) * SIDE + n // NZ

        @pl.when(i > 0)
        def _():
            slot_copy(i, me.tile).wait_recv()

        me.slot_math(i)
        return carry

    lax.fori_loop(0, SLOTS, step, 0)
    me.result()

    def finish(i, carry):
        slot_copy(i, me.tile).wait_send()
        return carry

    lax.fori_loop(1, SLOTS, finish, 0)
    for i in range(1, NG):
        me.bg_copy(i).wait_send()


def pick_step(m, table):
    value = table[-1]
    for k in range(len(table) - 2, -1, -1):
        value = jnp.where(m == k, table[k], value)
    return value


LATENTS_BY = (0, 0, 2, 4, 6, 8, 8, 8, 8, 8, 8, 8, 8)
SLOTS_BY = (0, 0, 0, 0, 2, 4, 8, 8, 16, 20, 24, 24)
GROUPS_BY = (1, 1, 1, 1, 1, 1, 3, 3, 3, 5, 5, 8)


def relay_kernel(table, *refs):
    hbm, out_ref = refs[:8], refs[8]
    (held, leaving, landing, packed, send_sem, recv_sem, zsend_sem, zrecv_sem), work = refs[9:17], refs[17:]
    me = Parts(table, hbm, out_ref, work)
    loads = me.loads(held.at[pl.ds(0, OBS_BLOCKS)])
    for load in loads:
        load.start()
    barrier = pltpu.get_barrier_semaphore()
    ring = (me.at(1, 0, 0), me.at(-1, 0, 0))
    peers = [(t, me.grp) for t in ring]
    peers += [(me.at(0, o // NC, o % NC), me.grp) for o in range(1, SIDE)]
    peers += [(me.tile, (me.grp + i) % NG) for i in range(1, NG)]
    for peer in peers:
        pl.semaphore_signal(barrier, inc=1, device_id=peer, device_id_type=MESH)
    loads[0].wait()
    pl.semaphore_wait(barrier, len(peers))
    slot_copy = slot_copier(me, packed, send_sem, recv_sem)

    def ring_copy(d, m):
        return pltpu.make_async_remote_copy(
            src_ref=leaving.at[d, m],
            dst_ref=landing.at[d, m],
            send_sem=zsend_sem.at[d, m],
            recv_sem=zrecv_sem.at[d, m],
            device_id=(ring[d], me.grp),
            device_id_type=MESH,
        )

    def side_send(i, carry):
        block = held[table[2, i]]
        o = i % SIDE

        @pl.when(o == 0)
        def _():
            me.recv[i] = block

        @pl.when(o > 0)
        def _():
            packed[i] = block
            slot_copy(i, me.at(0, o // NC, o % NC)).start()

        return carry

    def slot_step(i, carry):
        @pl.when(i % SIDE > 0)
        def _():
            slot_copy(i, me.tile).wait_recv()

        me.slot_math(i)
        return carry

    def step(m, carry):
        @pl.when(m >= 2)
        def _():
            for d in range(2):
                ring_copy(d, m - 2).wait_recv()
                for k in range(CHUNK):
                    held[OBS_BLOCKS + d * TURNS + (m - 2) * CHUNK + k] = landing[d, m - 2, k]

        @pl.when(m < CHUNKS)
        def _():
            for d in range(2):
                for k in range(CHUNK):
                    leaving[d, m, k] = held[table[d, m * CHUNK + k]]
                ring_copy(d, m).start()

        lax.fori_loop(
            jnp.where(m == 0, 0, pick_step(m - 1, GROUPS_BY)) * SIDE, pick_step(m, GROUPS_BY) * SIDE, side_send, 0
        )

        @pl.when(m == 1)
        def _():
            for load in loads[1:]:
                load.wait()
            for i in range(1, NG):
                me.bg_copy(i).start()
            me.setup()

        @pl.when(m == 3)
        def _():
            for i in range(1, NG):
                me.bg_copy(i).wait_recv()

        lax.fori_loop(jnp.where(m == 0, 0, pick_step(m - 1, LATENTS_BY)), pick_step(m, LATENTS_BY), me.latent_step, 0)
        lax.fori_loop(jnp.where(m == 0, 0, pick_step(m - 1, SLOTS_BY)), pick_step(m, SLOTS_BY), slot_step, 0)
        return carry

    lax.fori_loop(0, CHUNKS + 2, step, 0)
    lax.fori_loop(SLOTS_BY[-1], SLOTS, slot_step, 0)
    me.result()

    def finish(i, carry):
        @pl.when(i % SIDE > 0)
        def _():
            slot_copy(i, me.tile).wait_send()

        return carry

    lax.fori_loop(0, SLOTS, finish, 0)

    def ring_finish(m, carry):
        for d in range(2):
            ring_copy(d, m).wait_send()
        return carry

    lax.fori_loop(0, CHUNKS, ring_finish, 0)
    for i in range(1, NG):
        me.bg_copy(i).wait_send()


def exchange_call(kernel, collective_id, own_scratch, name):
    bf16, f32 = jnp.bfloat16, jnp.float32
    smem = pl.BlockSpec(memory_space=pltpu.SMEM)
    vmem = pl.BlockSpec(memory_space=pltpu.VMEM)
    hbm = pl.BlockSpec(memory_space=pl.ANY)
    shared = [
        pltpu.VMEM((SLOTS, BLOCK, CHANNELS), bf16),
        pltpu.VMEM((NG, 2 * BLOCK, WIDTH), bf16),
        pltpu.VMEM((CHANNELS, WIDTH), bf16),
        pltpu.VMEM((CHANNELS, WIDTH), bf16),
        pltpu.VMEM((WIDTH, WIDTH), bf16),
        pltpu.VMEM((WIDTH, WIDTH), bf16),
        pltpu.VMEM((WIDTH, WIDTH), bf16),
        pltpu.VMEM((WIDTH, WIDTH), bf16),
        pltpu.VMEM((2, PAIRS, 2 * HDIM, 2 * BLOCK), bf16),
        pltpu.VMEM((WIDTH, CHANNELS), bf16),
        pltpu.VMEM((WIDTH, WIDTH), bf16),
        pltpu.VMEM((2, HEADS, HDIM, BLOCK), f32),
        pltpu.VMEM((2, PAIRS, 8, 2 * BLOCK), f32),
        pltpu.SemaphoreType.DMA((8,)),
        pltpu.SemaphoreType.DMA((NG - 1,)),
        pltpu.SemaphoreType.DMA((NG - 1,)),
    ]
    return pl.pallas_call(
        kernel,
        out_shape=jax.ShapeDtypeStruct((2 * BLOCK, WIDTH), bf16),
        in_specs=[smem] + [hbm] * 8,
        out_specs=vmem,
        scratch_shapes=own_scratch + shared,
        compiler_params=pltpu.CompilerParams(
            collective_id=collective_id, has_side_effects=True, vmem_limit_bytes=48 * 1024 * 1024
        ),
        cost_estimate=pl.CostEstimate(flops=12_000_000_000, bytes_accessed=8_000_000, transcendentals=21_000_000),
        name=name,
    )


def slots_of(count):
    return pltpu.VMEM((count, BLOCK, CHANNELS), jnp.bfloat16)


def local(
    observations,
    obs_key_weight,
    obs_value_weight,
    background,
    query_weight,
    key_weight,
    value_weight,
    out_weight,
    owners,
    attend_list,
    obs_count,
):
    vmem = pl.BlockSpec(memory_space=pltpu.VMEM)
    table = pl.pallas_call(
        plan_kernel,
        out_shape=jax.ShapeDtypeStruct((8, RING), jnp.int32),
        in_specs=[pl.BlockSpec(memory_space=pltpu.SMEM), vmem, vmem],
        out_specs=vmem,
        name="plan",
    )(attend_list, owners.T, obs_count[None, :])
    dma = pltpu.SemaphoreType.DMA
    relay = exchange_call(
        relay_kernel,
        0,
        [
            slots_of(OBS_BLOCKS + 2 * TURNS),
            pltpu.VMEM((2, CHUNKS, CHUNK, BLOCK, CHANNELS), jnp.bfloat16),
            pltpu.VMEM((2, CHUNKS, CHUNK, BLOCK, CHANNELS), jnp.bfloat16),
            slots_of(SLOTS),
            dma((SLOTS,)),
            dma((SLOTS,)),
            dma((2, CHUNKS)),
            dma((2, CHUNKS)),
        ],
        "relay",
    )
    direct = exchange_call(
        direct_kernel, 1, [slots_of(OBS_BLOCKS), slots_of(SLOTS), dma((SLOTS,)), dma((SLOTS,))], "direct"
    )
    operands = (
        table,
        observations.reshape(OBS_BLOCKS, BLOCK, CHANNELS),
        obs_key_weight,
        obs_value_weight,
        background,
        query_weight,
        key_weight,
        value_weight,
        out_weight,
    )
    return lax.cond(table[5, 0] <= 0, lambda *a: relay(*a), lambda *a: direct(*a), *operands)


def solution(mesh):
    rows = P(("tile", "grp"), None)
    in_specs = (rows, P(), P(), rows, P(), P(), P(), P(), P(), rows, P())
    return jax.shard_map(local, mesh=mesh, in_specs=in_specs, out_specs=rows, check_vma=False)
```

time: 244 us -> 106 us (0.43)
  Pallas kernels: 0 us -> 104 us
  waiting for transfers between devices: 80.4 us -> 0 us
  local copies, waits for them, and re-layouts: 80.4 us -> 1.22 us
  matrix products: 49.2 us -> 0 us
  starting transfers between devices: 13.3 us -> 0 us
  between operations: 13.7 us -> 0.67 us
  other arithmetic: 5.07 us -> 0 us
    pallas_call x0 -> x2, Pallas kernels: none -> 104 us  [the longest x1 102 us: local(): relay(*a)]
    all_to_all x1 -> x0, waiting for transfers between devices: 56.5 us -> none  [local(): lax.all_to_all(packed, 'tile', split_axis=0, concat_axis=0, tiled=True)]
    gather x11 -> x0, local copies, waits for them, and re-layouts: 53.1 us -> none  [the longest x8 51.6 us: one_piece(): jnp.take(received, chosen, axis=0)]
    dot_general x23 -> x0, matrix products: 49.2 us -> none  [the longest x9 19.1 us: attend_piece(): jnp.einsum('rhe,khe->hrk', queries, all_keys, preferred_element_type=jnp....]
    all_gather x1 -> x0, waiting for transfers between devices: 23.3 us -> none  [local(): lax.all_gather(background, 'grp', axis=0, tiled=True)]
    while x48 -> x0, local copies, waits for them, and re-layouts: 16.5 us -> none
    all_to_all x1 -> x0, starting transfers between devices: 13.3 us -> none  [local(): lax.all_to_all(packed, 'tile', split_axis=0, concat_axis=0, tiled=True)]
    dot_general x1 -> x0, local copies, waits for them, and re-layouts: 4.37 us -> none  [local(): jnp.einsum('ks,kx->sx', placing, observations.reshape(obs_blocks, BLOCK *...]
  transfers between devices with their start and end apart: 2 -> 0, of which waited for: 2 -> 0; matrix products, arithmetic and copies ran while one was open for 6% -> 0% of each run, Pallas kernels for 0% -> 0%
where the time goes in v2:
time: 106 us; the launch traced here: 105 us
  Pallas kernels  104 us (98%)
  local copies, waits for them, and re-layouts  1.22 us (1%)
    pallas_call x1, Pallas kernels, local(): relay(*a)  102 us

profile of v2, /device:TPU:1, one launch (start us, length us, event | category | flops | bytes accessed | tf_op | source)
XLA Modules:
  0.0 105.4 jit_solution(18154637866962989940)
XLA Ops:
  0.0 1.6 %plan.1 = s32[8,256]{1,0:T(8,128)S(1)} custom-call(s32[2,32]{1,0:T(2,128)} %list_ref.1, s32[32,256]{1,0:T(8,128)} %bitcast.4, s32[1,256]{1,0:T(1,128)} %bitcast.5), custom_call_target="tpu_custom_call" | custom-call | tf_op jit(solution)/shard_map/plan/pallas_call | solution.py:502
  1.6 0.5 slice.4
  2.8 101.9 %conditional.1 = (bf16[256,512]{1,0:T(8,128)(2,1)S(1)}) conditional(s32[]{:T(128)} %bitcast.2, (s32[8,256]{1,0:T(8,128)S(1)}, bf16[32,128,256]{2,1,0:T(8,128)(2,1)}, bf16[256,512]{1,0:T(8,128)(2,1)}, bf16[256,512]{1,0:T(8,128)(2,1)}, bf16[256,512]{1,0:T(8,128)(2,1)}, /*index=5*/bf16[512,512]{1,0:T(8,128)(2,1)}, bf16[512,512]{1,0:T(8,128)(2,1)}, ...), branch_computations={%region_0.0_spmd, %region_1.0_spmd} | conditional | flops 12000000000 | bytes 8000008 | solution.py:539
  2.8 101.9 %relay.1 = bf16[256,512]{1,0:T(8,128)(2,1)S(1)} custom-call(s32[8,256]{1,0:T(8,128)S(1)} %get-tuple-element.53.table, bf16[32,128,256]{2,1,0:T(8,128)(2,1)} %get-tuple-element.54.refs_0_, bf16[256,512]{1,0:T(8,128)(2,1)} %get-tuple-element.55.refs_1_, bf16[256,512]{1,0:T(8,128)(2,1)} %get-tuple-element.56.refs_2_, ...), custom_call_target="tpu_custom_call" | custom-call | flops 12000000000 | bytes 8000000 | tf_op jit(solution)/shard_map/cond/branch_1_fun/relay/pallas_call | solution.py:539
  104.7 0.7 copy.17

commit v3 on v2

--- a/solution.py
+++ b/solution.py
@@ -22,11 +22,13 @@
 RING = SLOTS * NG
 STRIDE = RING // NZ
 OBS_BLOCKS = 32
-CHUNK = 4
-CHUNKS = 10
+CHUNK = 2
+CHUNKS = 20
+BEHIND = 3
 TURNS = CHUNK * CHUNKS
-LAG = 2 * CHUNK
-BOUNDS = (20, 32, 40, 40)
+LAG = BEHIND * CHUNK
+BOUNDS = (20, 30, 38, 40)
+BATCH = 4
 MESH = pl.DeviceIdType.MESH
 NT = (((1,), (1,)), ((), ()))
 
@@ -50,7 +52,16 @@
     away = (owners // (NX * NC) - lane // STRIDE + NZ) % NZ
     side = (owners // NC) % NX
     core = owners % NC
-    right = (away >= 1) & ((away < NZ // 2) | ((away == NZ // 2) & ((side + core) % 2 == 0)))
+    half = NZ // 2
+    middle = live & (away == half)
+    spare = tally(live & (away > half)) - tally(live & (away >= 1) & (away < half)) + tally(middle)
+    share = jnp.floor((spare + (lane_row % 2).astype(f32)) * 0.5)
+    seat, taken = side * NC + core, jnp.zeros((1, RING), f32)
+    earlier = jnp.zeros((n_blk, RING), f32)
+    for k in range(NX * NC):
+        earlier = jnp.where(seat == k, taken, earlier)
+        taken += tally(middle & (seat == k))
+    right = (away >= 1) & ((away < half) | ((away == half) & (earlier < share)))
     left = (away >= NZ // 2) & jnp.logical_not(right)
     hops = jnp.where(right, away, jnp.where(left, NZ - away, 0))
     moving = live & (hops > 0)
@@ -181,25 +192,29 @@
         self.acc[...] = jnp.zeros_like(self.acc)
         self.tot[...] = jnp.zeros_like(self.tot)
 
-    def attend(self, keys, vt, mask_rows, p, pick):
+    def weights(self, keys, p, pick):
         s = f32dot(keys[:, p * 2 * HDIM : (p + 1) * 2 * HDIM], self.qbd[pick, p])
         capped = jnp.tanh(s * (1.0 / (8.0 * SOFT_LIMIT)))
-        w = jnp.exp2(capped * (SOFT_LIMIT * LOG2E)).astype(jnp.bfloat16)
-        va = jnp.concatenate([vt[p * 2 * HDIM : (p + 1) * 2 * HDIM], mask_rows], axis=0)
-        o = f32dot(va, w)
+        return jnp.exp2(capped * (SOFT_LIMIT * LOG2E)).astype(jnp.bfloat16)
+
+    def mix(self, vt, mask_rows, w, p):
+        o = f32dot(jnp.concatenate([vt[p * 2 * HDIM : (p + 1) * 2 * HDIM], mask_rows], axis=0), w)
         return o[:HDIM, :BLOCK], o[HDIM : 2 * HDIM, BLOCK:], o[2 * HDIM : 2 * HDIM + 8]
 
+    def add(self, b, p, terms):
+        self.acc[b, 2 * p] += sum(t[0] for t in terms)
+        self.acc[b, 2 * p + 1] += sum(t[1] for t in terms)
+        self.tot[b, p] += sum(t[2] for t in terms)
+
     def latent_step(self, j, carry):
-        rows = self.bgs[j // 2, pl.ds(pl.multiple_of((j % 2) * BLOCK, BLOCK), BLOCK), :]
+        rows = self.bgs[j]
         keys = f32dot(rows, self.kw[...]).astype(jnp.bfloat16)
         vt = f32dot_nt(self.vwt[...], rows).astype(jnp.bfloat16)
-        ones = jnp.ones((16, BLOCK), jnp.bfloat16)
-        for b in range(2):
-            for p in range(PAIRS):
-                top, low, total = self.attend(keys, vt, ones, p, b)
-                self.acc[b, 2 * p] += top
-                self.acc[b, 2 * p + 1] += low
-                self.tot[b, p] += total
+        ones = jnp.ones((16, 2 * BLOCK), jnp.bfloat16)
+        ws = {(b, p): self.weights(keys, p, b) for p in range(PAIRS) for b in range(2)}
+        for p in range(PAIRS):
+            for b in range(2):
+                self.add(b, p, [self.mix(vt, ones, ws[b, p], p)])
         return carry
 
     def slot_way(self, i):
@@ -207,26 +222,27 @@
         dz = jnp.where(g % 2 == 1, (g + 1) // 2, (NZ - g // 2) % NZ)
         return dz, o // NC, o % NC
 
-    def slot_math(self, i):
-        dz, dx, dc = self.slot_way(i)
-        source = self.at(-dz, -dx, -dc)
-        rows_ok = self.table[3, source * NG + self.grp]
-        pick = self.table[4, source]
-        row_id = lax.broadcasted_iota(jnp.int32, (BLOCK, CHANNELS), 0)
-        block = self.recv[i]
-        block = jnp.where(row_id < rows_ok, block, jnp.zeros_like(block))
-        lane_id = lax.broadcasted_iota(jnp.int32, (16, BLOCK), 1)
-        mask_rows = jnp.where(lane_id < rows_ok, 1.0, 0.0).astype(jnp.bfloat16)
-        keys = f32dot(block, self.okw[...]).astype(jnp.bfloat16)
-        vt = f32dot_nt(self.ovwt[...], block).astype(jnp.bfloat16)
-        first = pick == 0
+    def slot_math(self, first):
+        picks, blocks, masks = [], [], []
+        for k in range(BATCH):
+            dz, dx, dc = self.slot_way(first + k)
+            source = self.at(-dz, -dx, -dc)
+            rows_ok = self.table[3, source * NG + self.grp]
+            picks.append(self.table[4, source])
+            row_id = lax.broadcasted_iota(jnp.int32, (BLOCK, CHANNELS), 0)
+            block = self.recv[first + k]
+            blocks.append(jnp.where(row_id < rows_ok, block, jnp.zeros_like(block)))
+            lane_id = lax.broadcasted_iota(jnp.int32, (16, BLOCK), 1)
+            masks.append(jnp.where(lane_id < rows_ok, 1.0, 0.0).astype(jnp.bfloat16))
+        rows = jnp.concatenate(blocks, axis=0)
+        keys = f32dot(rows, self.okw[...]).astype(jnp.bfloat16)
+        vt = f32dot_nt(self.ovwt[...], rows).astype(jnp.bfloat16)
+        part = [slice(k * BLOCK, (k + 1) * BLOCK) for k in range(BATCH)]
+        ws = {(p, k): self.weights(keys[part[k]], p, picks[k]) for p in range(PAIRS) for k in range(BATCH)}
         for p in range(PAIRS):
-            top, low, total = self.attend(keys, vt, mask_rows, p, pick)
+            terms = [self.mix(vt[:, part[k]], masks[k], ws[p, k], p) for k in range(BATCH)]
             for b in range(2):
-                mine = first if b == 0 else jnp.logical_not(first)
-                self.acc[b, 2 * p] += jnp.where(mine, top, 0.0)
-                self.acc[b, 2 * p + 1] += jnp.where(mine, low, 0.0)
-                self.tot[b, p] += jnp.where(mine, total, 0.0)
+                self.add(b, p, [[jnp.where(picks[k] == b, v, 0.0) for v in terms[k]] for k in range(BATCH)])
 
     def result(self):
         for b in range(2):
@@ -278,8 +294,7 @@
     for i in range(1, NG):
         me.bg_copy(i).start()
 
-    def send(n, carry):
-        i = (n % NZ) * SIDE + n // NZ
+    def send(i, carry):
         dest = me.at(*me.slot_way(i))
         block = held[table[6, dest]]
 
@@ -298,19 +313,19 @@
     me.setup()
     for i in range(1, NG):
         me.bg_copy(i).wait_recv()
-    lax.fori_loop(0, 2 * NG, me.latent_step, 0)
+    lax.fori_loop(0, NG, me.latent_step, 0)
 
     def step(n, carry):
-        i = (n % NZ) * SIDE + n // NZ
-
-        @pl.when(i > 0)
-        def _():
-            slot_copy(i, me.tile).wait_recv()
-
-        me.slot_math(i)
-        return carry
-
-    lax.fori_loop(0, SLOTS, step, 0)
+        for k in range(BATCH):
+
+            @pl.when(n * BATCH + k > 0)
+            def _():
+                slot_copy(n * BATCH + k, me.tile).wait_recv()
+
+        me.slot_math(n * BATCH)
+        return carry
+
+    lax.fori_loop(0, SLOTS // BATCH, step, 0)
     me.result()
 
     def finish(i, carry):
@@ -322,16 +337,13 @@
         me.bg_copy(i).wait_send()
 
 
-def pick_step(m, table):
-    value = table[-1]
-    for k in range(len(table) - 2, -1, -1):
-        value = jnp.where(m == k, table[k], value)
-    return value
-
-
-LATENTS_BY = (0, 0, 2, 4, 6, 8, 8, 8, 8, 8, 8, 8, 8)
-SLOTS_BY = (0, 0, 0, 0, 2, 4, 8, 8, 16, 20, 24, 24)
-GROUPS_BY = (1, 1, 1, 1, 1, 1, 3, 3, 3, 5, 5, 8)
+def reached(m, marks):
+    return sum(jnp.where(m >= mark, 1, 0) for mark in marks)
+
+
+LATENT_MARKS = (3, 5, 6, 7)
+BATCH_MARKS = (8, 9, 15, 16, 17, 18, 20)
+GROUP_MARKS = (0, 12, 12, 17, 17, 21, 21, 22)
 
 
 def relay_kernel(table, *refs):
@@ -377,21 +389,23 @@
 
         return carry
 
-    def slot_step(i, carry):
-        @pl.when(i % SIDE > 0)
-        def _():
-            slot_copy(i, me.tile).wait_recv()
-
-        me.slot_math(i)
+    def slot_step(n, carry):
+        for k in range(BATCH):
+
+            @pl.when((n * BATCH + k) % SIDE > 0)
+            def _():
+                slot_copy(n * BATCH + k, me.tile).wait_recv()
+
+        me.slot_math(n * BATCH)
         return carry
 
     def step(m, carry):
-        @pl.when(m >= 2)
+        @pl.when(m >= BEHIND)
         def _():
             for d in range(2):
-                ring_copy(d, m - 2).wait_recv()
+                ring_copy(d, m - BEHIND).wait_recv()
                 for k in range(CHUNK):
-                    held[OBS_BLOCKS + d * TURNS + (m - 2) * CHUNK + k] = landing[d, m - 2, k]
+                    held[OBS_BLOCKS + d * TURNS + (m - BEHIND) * CHUNK + k] = landing[d, m - BEHIND, k]
 
         @pl.when(m < CHUNKS)
         def _():
@@ -400,9 +414,7 @@
                     leaving[d, m, k] = held[table[d, m * CHUNK + k]]
                 ring_copy(d, m).start()
 
-        lax.fori_loop(
-            jnp.where(m == 0, 0, pick_step(m - 1, GROUPS_BY)) * SIDE, pick_step(m, GROUPS_BY) * SIDE, side_send, 0
-        )
+        lax.fori_loop(reached(m - 1, GROUP_MARKS) * SIDE, reached(m, GROUP_MARKS) * SIDE, side_send, 0)
 
         @pl.when(m == 1)
         def _():
@@ -412,17 +424,17 @@
                 me.bg_copy(i).start()
             me.setup()
 
-        @pl.when(m == 3)
+        @pl.when(m == LATENT_MARKS[1])
         def _():
             for i in range(1, NG):
                 me.bg_copy(i).wait_recv()
 
-        lax.fori_loop(jnp.where(m == 0, 0, pick_step(m - 1, LATENTS_BY)), pick_step(m, LATENTS_BY), me.latent_step, 0)
-        lax.fori_loop(jnp.where(m == 0, 0, pick_step(m - 1, SLOTS_BY)), pick_step(m, SLOTS_BY), slot_step, 0)
-        return carry
-
-    lax.fori_loop(0, CHUNKS + 2, step, 0)
-    lax.fori_loop(SLOTS_BY[-1], SLOTS, slot_step, 0)
+        lax.fori_loop(reached(m - 1, LATENT_MARKS), reached(m, LATENT_MARKS), me.latent_step, 0)
+        lax.fori_loop(reached(m - 1, BATCH_MARKS), reached(m, BATCH_MARKS), slot_step, 0)
+        return carry
+
+    lax.fori_loop(0, CHUNKS + BEHIND, step, 0)
+    lax.fori_loop(len(BATCH_MARKS), SLOTS // BATCH, slot_step, 0)
     me.result()
 
     def finish(i, carry):

time: 106 us -> 93.3 us (0.88)
  Pallas kernels: 104 us -> 91.3 us
    pallas_call x1, Pallas kernels: 102 us -> 89.6 us  [local(): relay(*a)]
where the time goes in v3:
time: 93.3 us; the launch traced here: 93.2 us
  Pallas kernels  91.3 us (98%)
  local copies, waits for them, and re-layouts  1.22 us (1%)
    pallas_call x1, Pallas kernels, local(): relay(*a)  89.6 us

profile of v3, /device:TPU:1, one launch (start us, length us, event | category | flops | bytes accessed | tf_op | source)
XLA Modules:
  0.0 93.2 jit_solution(3427921188479806881)
XLA Ops:
  0.0 1.7 %plan.1 = s32[8,256]{1,0:T(8,128)S(1)} custom-call(s32[2,32]{1,0:T(2,128)} %list_ref.1, s32[32,256]{1,0:T(8,128)} %bitcast.4, s32[1,256]{1,0:T(1,128)} %bitcast.5), custom_call_target="tpu_custom_call" | custom-call | tf_op jit(solution)/shard_map/plan/pallas_call | solution.py:514
  1.7 0.5 slice.4
  2.8 89.6 %conditional.1 = (bf16[256,512]{1,0:T(8,128)(2,1)S(1)}) conditional(s32[]{:T(128)} %bitcast.2, (s32[8,256]{1,0:T(8,128)S(1)}, bf16[32,128,256]{2,1,0:T(8,128)(2,1)}, bf16[256,512]{1,0:T(8,128)(2,1)}, bf16[256,512]{1,0:T(8,128)(2,1)}, bf16[256,512]{1,0:T(8,128)(2,1)}, /*index=5*/bf16[512,512]{1,0:T(8,128)(2,1)}, bf16[512,512]{1,0:T(8,128)(2,1)}, ...), branch_computations={%region_0.0_spmd, %region_1.0_spmd} | conditional | flops 12000000000 | bytes 8000008 | solution.py:551
  2.9 89.6 %relay.1 = bf16[256,512]{1,0:T(8,128)(2,1)S(1)} custom-call(s32[8,256]{1,0:T(8,128)S(1)} %get-tuple-element.53.table, bf16[32,128,256]{2,1,0:T(8,128)(2,1)} %get-tuple-element.54.refs_0_, bf16[256,512]{1,0:T(8,128)(2,1)} %get-tuple-element.55.refs_1_, bf16[256,512]{1,0:T(8,128)(2,1)} %get-tuple-element.56.refs_2_, ...), custom_call_target="tpu_custom_call" | custom-call | flops 12000000000 | bytes 8000000 | tf_op jit(solution)/shard_map/cond/branch_1_fun/relay/pallas_call | solution.py:551
  92.5 0.7 copy.17

commit v4 on v3

--- a/solution.py
+++ b/solution.py
@@ -27,7 +27,12 @@
 BEHIND = 3
 TURNS = CHUNK * CHUNKS
 LAG = BEHIND * CHUNK
-BOUNDS = (20, 30, 38, 40)
+FAR = 3
+EARLY_DZ = (FAR, NZ - FAR)
+EARLY = 4
+EARLY_STEP = 6
+ORDER = (("own", 1), ("early", 1), ("own", 2), ("early", 2), ("own", 3), ("early", 3), ("own", 4))
+BOUNDS = {("own", 1): 18, ("own", 2): 28, ("own", 3): 36}
 BATCH = 4
 MESH = pl.DeviceIdType.MESH
 NT = (((1,), (1,)), ((), ()))
@@ -53,8 +58,11 @@
     side = (owners // NC) % NX
     core = owners % NC
     half = NZ // 2
-    middle = live & (away == half)
-    spare = tally(live & (away > half)) - tally(live & (away >= 1) & (away < half)) + tally(middle)
+    ahead_of_z = (side - lane // (NC * NG) + 2 * NX) % NX == NX // 2
+    early = ahead_of_z & ((away == FAR) | (away == NZ - FAR))
+    going = live & (away > 0) & jnp.logical_not(early)
+    middle = going & (away == half)
+    spare = tally(going & (away > half)) - tally(going & (away < half)) + tally(middle)
     share = jnp.floor((spare + (lane_row % 2).astype(f32)) * 0.5)
     seat, taken = side * NC + core, jnp.zeros((1, RING), f32)
     earlier = jnp.zeros((n_blk, RING), f32)
@@ -64,7 +72,7 @@
     right = (away >= 1) & ((away < half) | ((away == half) & (earlier < share)))
     left = (away >= NZ // 2) & jnp.logical_not(right)
     hops = jnp.where(right, away, jnp.where(left, NZ - away, 0))
-    moving = live & (hops > 0)
+    moving = going
     shift = (side - (lane // (NC * NG)) % NX + NX + NX - 1) % NX
     order = (4 - hops) * (NX * NC) + shift * NC + core + jnp.where(right, 0, 64)
     key = jnp.where(moving, order, 1000)
@@ -72,28 +80,65 @@
     for k in range(n_blk):
         other = key[k : k + 1]
         rank += jnp.where((other < key) & ((other < 64) == (key < 64)), 1.0, 0.0)
-    ahead, starts, over = {}, {}, jnp.zeros((1, RING), f32)
+    my_core = (lane_row // NG) % NC
+    my_side = (lane_row // (NC * NG)) % NX
+    hop_lanes = NC * NG * (NX // 2)
+
+    def across(v):
+        return jnp.where(my_side < NX // 2, roll(v, -hop_lanes), roll(v, hop_lanes))
+
+    def sibling(v):
+        return jnp.where(my_core == 0, roll(v, -NG), roll(v, NG))
+
+    blockf = block.astype(f32)
+    flag, early_idx = {}, []
+    for dz in EARLY_DZ:
+        sent = []
+        for dest_core in range(NC):
+            hit = live & early & (away == dz) & (core == dest_core)
+            sent.append(across(tally(hit)))
+            early_idx.append(jnp.sum(jnp.where(hit, blockf, 0.0), axis=0, keepdims=True))
+        flag[dz, 0] = jnp.where(my_core == 0, sent[0], sent[1])
+        flag[dz, 1] = jnp.where(my_core == 0, sibling(sent[0]), sibling(sent[1]))
+    early_list = tuple(tuple((dz, dc) for dc in range(NC)) for dz in EARLY_DZ)
+    lengths, starts, over = {}, {}, jnp.zeros((1, RING), f32)
     for d, way in enumerate((right, left)):
         turn = 1 if d == 0 else -1
-        count = [tally(moving & way & (hops >= k)) for k in range(1, 5)]
-        begin = [jnp.zeros((1, RING), f32)]
-        for k in range(1, 4):
-            length = roll(count[k - 1], turn * (k - 1) * STRIDE)
-            begin.append(jnp.maximum(begin[-1] + length, roll(begin[-1], turn * STRIDE) + LAG))
-        for k in range(4):
-            length = roll(count[k], turn * k * STRIDE)
-            over = jnp.maximum(over, begin[k] + length - BOUNDS[k])
-            ahead[d, k] = length
-            starts[d, k] = begin[k]
+        far = flag[early_list[d][0]] + flag[early_list[d][1]]
+        position = jnp.zeros((1, RING), f32)
+        for kind, k in ORDER:
+            if kind == "own":
+                count = tally(moving & way & (hops >= k))
+            else:
+                count = far
+            length = roll(count, turn * (k - 1) * STRIDE)
+            if k > 1:
+                begin = jnp.maximum(position, roll(starts[d, kind, k - 1], turn * STRIDE) + LAG)
+            else:
+                begin = jnp.maximum(position, EARLY_STEP * CHUNK if kind == "early" else 0)
+            position = jnp.where(length > 0, begin + length, position)
+            over = jnp.maximum(over, position - BOUNDS.get((kind, k), TURNS))
+            lengths[d, kind, k], starts[d, kind, k] = length, begin
+
+    def landed(d, kind, k):
+        return roll(starts[d, kind, k], (k if d else -k) * STRIDE + (STRIDE if d == 0 else -STRIDE))
+
     spot = jnp.zeros((n_blk, RING), f32)
     for d, way in enumerate((right, left)):
-        turn = 1 if d == 0 else -1
-        for k in range(4):
-            landed = roll(starts[d, k], -turn * k * STRIDE)
-            spot = jnp.where(way & (hops == k + 1), landed + rank + (n_blk + d * TURNS), spot)
-    blockf = block.astype(f32)
+        for k in range(1, 5):
+            spot = jnp.where(way & (hops == k), landed(d, "own", k) + rank + (n_blk + d * TURNS), spot)
     spot = jnp.where(hops == 0, blockf, spot)
-    spot = jnp.where(live, spot, -1.0)
+    spot = jnp.where(live & jnp.logical_not(early), spot, -1.0)
+    early_spot, first_early = {}, n_blk + 2 * TURNS
+    own_early = []
+    for d in range(2):
+        before = jnp.zeros((1, RING), f32)
+        chosen = []
+        for dz, dc in early_list[d]:
+            early_spot[dz, dc] = landed(d, "early", FAR) + before + (n_blk + d * TURNS)
+            chosen.append((flag[dz, dc], before, first_early + d * NC + dc))
+            before = before + flag[dz, dc]
+        own_early.append(chosen)
     rows = []
     turns = lane_row.astype(f32)
     own_key, own_rank = column(key.astype(f32), me), column(rank, me)
@@ -102,11 +147,16 @@
         mine = (own_key < 64.0) if d == 0 else ((own_key >= 64.0) & (own_key < 1000.0))
         source = jnp.sum(jnp.where(mine & (own_rank == turns), blockf, 0.0), axis=0, keepdims=True)
         before = (me - turn * STRIDE + RING) % RING
-        for k in range(1, 4):
-            begin, length = column(starts[d, k], me), column(ahead[d, k], me)
-            old = column(starts[d, k - 1], before)
-            inside = (turns >= begin) & (turns < begin + length)
-            source = jnp.where(inside, turns - begin + old + (n_blk + d * TURNS), source)
+        begin = column(starts[d, "early", 1], me)
+        for here, seat_no, held_at in own_early[d]:
+            at = begin + column(seat_no, me)
+            source = jnp.where((column(here, me) > 0) & (turns == at), float(held_at), source)
+        for kind, k in ORDER:
+            if k > 1:
+                begin, length = column(starts[d, kind, k], me), column(lengths[d, kind, k], me)
+                old = column(starts[d, kind, k - 1], before)
+                inside = (turns >= begin) & (turns < begin + length)
+                source = jnp.where(inside, turns - begin + old + (n_blk + d * TURNS), source)
         rows.append(source)
     group = lane_row // (NX * NC)
     owner_cols = jnp.zeros((n_blk, RING), f32)
@@ -120,7 +170,14 @@
     local = lane_row % (NX * NC)
     dest = (z * NX + (x + local // NC) % NX) * NC + (c + local % NC) % NC
     found = (owner_cols == dest.astype(f32)) & (spot_cols >= 0.0)
-    rows.append(jnp.sum(jnp.where(found, spot_cols, 0.0), axis=0, keepdims=True))
+    place = jnp.sum(jnp.where(found, spot_cols, 0.0), axis=0, keepdims=True)
+    for dz in EARLY_DZ:
+        g = 2 * dz - 1 if dz <= half else 2 * (NZ - dz)
+        origin = (me - dz * STRIDE + RING) % RING
+        for dc in range(NC):
+            lands = column(jnp.where(flag[dz, dc] > 0, early_spot[dz, dc], 0.0), origin)
+            place = jnp.where(lane_row == g * SIDE + (NX // 2) * NC + dc, lands, place)
+    rows.append(place)
     limits = jnp.clip(counts - block * BLOCK, 0, BLOCK).astype(f32)
     rows.append(jnp.sum(jnp.where(owners == tile, limits, 0.0), axis=0, keepdims=True))
     pick = jnp.zeros((1, RING), f32)
@@ -130,7 +187,10 @@
     rows.append(jnp.broadcast_to(jnp.max(over, axis=1, keepdims=True), (1, RING)))
     own_owner = column(ownersf, me)
     rows.append(jnp.sum(jnp.where(own_owner == turns, blockf, 0.0), axis=0, keepdims=True))
-    rows.append(jnp.zeros((1, RING), f32))
+    early_row = jnp.zeros((1, RING), f32)
+    for k, idx in enumerate(early_idx):
+        early_row = jnp.where(lane_row == k, column(idx, me), early_row)
+    rows.append(early_row)
     return jnp.concatenate(rows, axis=0).astype(i32)
 
 
@@ -342,13 +402,14 @@
 
 
 LATENT_MARKS = (3, 5, 6, 7)
-BATCH_MARKS = (8, 9, 15, 16, 17, 18, 20)
-GROUP_MARKS = (0, 12, 12, 17, 17, 21, 21, 22)
+BATCH_MARKS = (8, 9, 14, 15, 16, 17, 19, 20, 21)
+GROUP_MARKS = (0, 11, 11, 16, 16, 20, 20, 22)
 
 
 def relay_kernel(table, *refs):
     hbm, out_ref = refs[:8], refs[8]
-    (held, leaving, landing, packed, send_sem, recv_sem, zsend_sem, zrecv_sem), work = refs[9:17], refs[17:]
+    (held, leaving, landing, packed, ahead, ahead_in) = refs[9:15]
+    (send_sem, recv_sem, zsend_sem, zrecv_sem, asend_sem, arecv_sem), work = refs[15:21], refs[21:]
     me = Parts(table, hbm, out_ref, work)
     loads = me.loads(held.at[pl.ds(0, OBS_BLOCKS)])
     for load in loads:
@@ -374,6 +435,22 @@
             device_id_type=MESH,
         )
 
+    def early_copy(n):
+        return pltpu.make_async_remote_copy(
+            src_ref=ahead.at[n],
+            dst_ref=ahead_in.at[n],
+            send_sem=asend_sem.at[n],
+            recv_sem=arecv_sem.at[n],
+            device_id=(me.at(0, NX // 2, n % NC), me.grp),
+            device_id_type=MESH,
+        )
+
+    def stays(i):
+        return (i % SIDE == 0) | comes_early(i)
+
+    def comes_early(i):
+        return (i >= (2 * FAR - 1) * SIDE) & (i < (2 * FAR + 1) * SIDE) & ((i % SIDE) // NC == NX // 2)
+
     def side_send(i, carry):
         block = held[table[2, i]]
         o = i % SIDE
@@ -382,7 +459,7 @@
         def _():
             me.recv[i] = block
 
-        @pl.when(o > 0)
+        @pl.when(jnp.logical_not(stays(i)))
         def _():
             packed[i] = block
             slot_copy(i, me.at(0, o // NC, o % NC)).start()
@@ -392,7 +469,7 @@
     def slot_step(n, carry):
         for k in range(BATCH):
 
-            @pl.when((n * BATCH + k) % SIDE > 0)
+            @pl.when(jnp.logical_not(stays(n * BATCH + k)))
             def _():
                 slot_copy(n * BATCH + k, me.tile).wait_recv()
 
@@ -407,12 +484,25 @@
                 for k in range(CHUNK):
                     held[OBS_BLOCKS + d * TURNS + (m - BEHIND) * CHUNK + k] = landing[d, m - BEHIND, k]
 
+        @pl.when(m == EARLY_STEP)
+        def _():
+            for n in range(EARLY):
+                early_copy(n).wait_recv()
+                held[OBS_BLOCKS + 2 * TURNS + n] = ahead_in[n]
+
         @pl.when(m < CHUNKS)
         def _():
             for d in range(2):
                 for k in range(CHUNK):
                     leaving[d, m, k] = held[table[d, m * CHUNK + k]]
                 ring_copy(d, m).start()
+
+        @pl.when(m == 0)
+        def _():
+            for n in range(EARLY):
+                far, dc = n // NC, n % NC
+                ahead[n] = held[table[7, far * NC + (me.c + dc) % NC]]
+                early_copy(n).start()
 
         lax.fori_loop(reached(m - 1, GROUP_MARKS) * SIDE, reached(m, GROUP_MARKS) * SIDE, side_send, 0)
 
@@ -434,11 +524,15 @@
         return carry
 
     lax.fori_loop(0, CHUNKS + BEHIND, step, 0)
+    for g in (2 * FAR - 1, 2 * FAR):
+        for dc in range(NC):
+            i = g * SIDE + (NX // 2) * NC + dc
+            me.recv[i] = held[table[2, i]]
     lax.fori_loop(len(BATCH_MARKS), SLOTS // BATCH, slot_step, 0)
     me.result()
 
     def finish(i, carry):
-        @pl.when(i % SIDE > 0)
+        @pl.when(jnp.logical_not(stays(i)))
         def _():
             slot_copy(i, me.tile).wait_send()
 
@@ -452,6 +546,8 @@
         return carry
 
     lax.fori_loop(0, CHUNKS, ring_finish, 0)
+    for n in range(EARLY):
+        early_copy(n).wait_send()
     for i in range(1, NG):
         me.bg_copy(i).wait_send()
 
@@ -523,14 +619,18 @@
         relay_kernel,
         0,
         [
-            slots_of(OBS_BLOCKS + 2 * TURNS),
+            slots_of(OBS_BLOCKS + 2 * TURNS + EARLY),
             pltpu.VMEM((2, CHUNKS, CHUNK, BLOCK, CHANNELS), jnp.bfloat16),
             pltpu.VMEM((2, CHUNKS, CHUNK, BLOCK, CHANNELS), jnp.bfloat16),
             slots_of(SLOTS),
+            slots_of(EARLY),
+            slots_of(EARLY),
             dma((SLOTS,)),
             dma((SLOTS,)),
             dma((2, CHUNKS)),
             dma((2, CHUNKS)),
+            dma((EARLY,)),
+            dma((EARLY,)),
         ],
         "relay",
     )

time: 93.3 us -> 85.5 us (0.916)
  Pallas kernels: 91.3 us -> 83.4 us
    pallas_call x1, Pallas kernels: 89.6 us -> 81.5 us  [local(): relay(*a)]
where the time goes in v4:
time: 85.5 us; the launch traced here: 85.3 us
  Pallas kernels  83.4 us (98%)
  local copies, waits for them, and re-layouts  1.22 us (1%)
    pallas_call x1, Pallas kernels, local(): relay(*a)  81.5 us
    pallas_call x1, Pallas kernels, local(): pl.pallas_call(plan_kernel, out_shape=jax.ShapeDtypeStruct((8, RING), jnp...  1.93 us

profile of v4, /device:TPU:1, one launch (start us, length us, event | category | flops | bytes accessed | tf_op | source)
XLA Modules:
  0.0 85.3 jit_solution(1084971092904091563)
XLA Ops:
  0.0 1.9 %plan.1 = s32[8,256]{1,0:T(8,128)S(1)} custom-call(s32[2,32]{1,0:T(2,128)} %list_ref.1, s32[32,256]{1,0:T(8,128)} %bitcast.4, s32[1,256]{1,0:T(1,128)} %bitcast.5), custom_call_target="tpu_custom_call" | custom-call | tf_op jit(solution)/shard_map/plan/pallas_call | solution.py:610
  1.9 0.5 slice.4
  3.1 81.5 %conditional.1 = (bf16[256,512]{1,0:T(8,128)(2,1)S(1)}) conditional(s32[]{:T(128)} %bitcast.2, (s32[8,256]{1,0:T(8,128)S(1)}, bf16[32,128,256]{2,1,0:T(8,128)(2,1)}, bf16[256,512]{1,0:T(8,128)(2,1)}, bf16[256,512]{1,0:T(8,128)(2,1)}, bf16[256,512]{1,0:T(8,128)(2,1)}, /*index=5*/bf16[512,512]{1,0:T(8,128)(2,1)}, bf16[512,512]{1,0:T(8,128)(2,1)}, ...), branch_computations={%region_0.0_spmd, %region_1.0_spmd} | conditional | flops 12000000000 | bytes 8000008 | solution.py:651
  3.1 81.5 %relay.1 = bf16[256,512]{1,0:T(8,128)(2,1)S(1)} custom-call(s32[8,256]{1,0:T(8,128)S(1)} %get-tuple-element.53.table, bf16[32,128,256]{2,1,0:T(8,128)(2,1)} %get-tuple-element.54.refs_0_, bf16[256,512]{1,0:T(8,128)(2,1)} %get-tuple-element.55.refs_1_, bf16[256,512]{1,0:T(8,128)(2,1)} %get-tuple-element.56.refs_2_, ...), custom_call_target="tpu_custom_call" | custom-call | flops 12000000000 | bytes 8000000 | tf_op jit(solution)/shard_map/cond/branch_1_fun/relay/pallas_call | solution.py:651
  84.6 0.7 copy.17
